TPU v7x, 512 devices: a whole 4x8x8 slice. The times are simulated.
512 devices in a mesh: rows: 32 (over y, x), sub: 16 (over z, core).
Axes of the slice: x: 4, y: 8, z: 8, core: 2. Of those that a mesh axis runs over, the one named last changes fastest.
Arguments:
- slab: bfloat16 [131072, 1024], P(('rows', 'sub')), may hold values from -6 to 6
- lower_bound: float32 [1], replicated, may hold values from 0.3 to 0.7
Outputs:
- panel_out: float32 [131072, 1024], P(('rows', 'sub'))
- checksum_out: float32 [512, 1024], P(('rows', 'sub'))
All inputs are finite; a program needn't handle non-finite values.
Results may differ from a plain program's by a relative error of at most 0.0017.
The roundings to bfloat16 on the way count: a program that leaves them out, or rounds other values in their place, can miss the bound.
Values sent between devices are 32-bit elements; how exact they have to be, the bound alone decides.
No kernel may reach another device: no remote copies, remote signals or barrier semaphores. Data moves between devices by JAX's collectives and lax.ppermute only.
A program may use at most 128 MiB of HBM per device.

v0:
```python
import math

import jax
import jax.numpy as jnp
from jax import lax
from jax.sharding import PartitionSpec as P


def qdwh_weights(lower_bound):
    value = lower_bound[0]
    square = value * value
    delta = jnp.cbrt(4.0 * (1.0 - square) / (square * square))
    root = jnp.sqrt(1.0 + delta)
    alpha = root + 0.5 * jnp.sqrt(8.0 - 4.0 * delta + 8.0 * (2.0 - square) / (square * root))
    beta = (alpha - 1.0) ** 2 / 4.0
    shift = alpha + beta - 1.0
    return (beta / shift, alpha - beta / shift, shift)


def cross_product(upper, lower):
    return lax.dot_general(
        upper, lower, (((0,), (0,)), ((), ())), preferred_element_type=jnp.float32
    )


def exact_dot(left, right):
    return jnp.dot(left, right, precision=lax.Precision.HIGHEST)


def blocked_inverse_factor(shifted):
    width = shifted.shape[0]
    block_size = 256
    count = width // block_size
    factor_blocks = [[None] * count for _ in range(count)]
    trailing = shifted
    for column in range(count):
        diagonal = jnp.linalg.cholesky(trailing[:block_size, :block_size])
        factor_blocks[column][column] = diagonal
        if column + 1 < count:
            below = trailing[block_size:, :block_size]
            panel = lax.linalg.triangular_solve(
                diagonal, below, left_side=False, lower=True, transpose_a=True
            )
            trailing = trailing[block_size:, block_size:] - exact_dot(panel, panel.T)
            for later in range(column + 1, count):
                start = (later - column - 1) * block_size
                factor_blocks[later][column] = panel[start : start + block_size]
    eye_block = jnp.eye(block_size, dtype=jnp.float32)
    inverse_blocks = [[None] * count for _ in range(count)]
    for index in range(count):
        inverse_blocks[index][index] = lax.linalg.triangular_solve(
            factor_blocks[index][index], eye_block, left_side=True, lower=True
        )
    for gap in range(1, count):
        for column in range(count - gap):
            row_index = column + gap
            total = jnp.zeros((block_size, block_size), jnp.float32)
            for middle in range(column, row_index):
                total = total + exact_dot(
                    factor_blocks[row_index][middle], inverse_blocks[middle][column]
                )
            inverse_blocks[row_index][column] = -exact_dot(
                inverse_blocks[row_index][row_index], total
            )
    zero_block = jnp.zeros((block_size, block_size), jnp.float32)
    rows_list = []
    for row_index in range(count):
        pieces = [
            inverse_blocks[row_index][column] if column <= row_index else zero_block
            for column in range(count)
        ]
        rows_list.append(jnp.concatenate(pieces, axis=1))
    return jnp.concatenate(rows_list, axis=0)


def per_device(slab, lower_bound):
    rows_dev, width = slab.shape
    half = width // 2
    devices_all = lax.axis_size("rows") * lax.axis_size("sub")
    rows_all = rows_dev * devices_all
    left_panel = slab[:, :half]
    right_panel = slab[:, half:]
    block_one = cross_product(left_panel, left_panel)
    block_two = cross_product(right_panel, left_panel)
    block_three = cross_product(right_panel, right_panel)
    square_size = half * half
    terms = jnp.concatenate([block_one.reshape(-1), block_two.reshape(-1), block_three.reshape(-1)])
    shares = lax.psum_scatter(terms, ("rows", "sub"), scatter_dimension=0, tiled=True)
    summed = lax.all_gather(shares, ("rows", "sub"), axis=0, tiled=True)
    summed = summed / rows_all
    gram_one = summed[:square_size].reshape(half, half)
    gram_two = summed[square_size : 2 * square_size].reshape(half, half)
    gram_three = summed[2 * square_size :].reshape(half, half)
    gram = jnp.concatenate(
        [
            jnp.concatenate([gram_one, gram_two.T], axis=1),
            jnp.concatenate([gram_two, gram_three], axis=1),
        ],
        axis=0,
    )
    first, second, shift = qdwh_weights(lower_bound)
    identity = jnp.eye(width, dtype=jnp.float32)
    shifted = identity + shift * gram
    inverse = blocked_inverse_factor(shifted)
    inverse_half = inverse.astype(jnp.bfloat16)
    projected = jnp.dot(slab, inverse_half.T, preferred_element_type=jnp.float32).astype(
        jnp.bfloat16
    )
    solved = jnp.dot(projected, inverse_half, preferred_element_type=jnp.float32)
    panel_out = first * slab.astype(jnp.float32) + second * solved
    checksum = jnp.sum(slab.astype(jnp.float32), axis=0, keepdims=True) / math.sqrt(rows_dev)
    check_solved = jnp.dot(
        jnp.dot(checksum, inverse.T, precision=lax.Precision.HIGHEST),
        inverse,
        precision=lax.Precision.HIGHEST,
    )
    checksum_out = first * checksum + second * check_solved
    return (panel_out, checksum_out)


def solution(mesh):
    return jax.shard_map(
        per_device,
        mesh=mesh,
        in_specs=(P(("rows", "sub"), None), P()),
        out_specs=(P(("rows", "sub"), None), P(("rows", "sub"), None)),
        check_vma=False,
    )
```

profile of v0, /device:TPU:1, one launch (start us, length us, event | category | flops | bytes accessed | tf_op | source)
XLA Modules:
  0.0 785.1 jit_solution(12605321899991277658)
XLA Ops:
  7.2 1.4 convolution_bitcast_fusion.2
  8.6 1.4 convolution_bitcast_fusion.1
  9.9 1.4 convolution_bitcast_fusion
  12.1 1.9 pad_maximum_fusion
  14.1 287.4 %all-reduce.5.cloned.1.call-done = f32[786432]{0:T(1024)} async-done(((f32[786432]{0:T(1024)}), f32[786432]{0:T(1024)}) %all-reduce.5.cloned.1.call-update) | async-done | bytes 3145744
  304.0 117.0 %all-gather.3.cloned.1.call-done = f32[512,1,1536]{2,1,0:T(1,128)} async-done(((f32[1,1,1536]{2,1,0:T(1,128)}), f32[512,1,1536]{2,1,0:T(1,128)}) %all-gather.3.cloned.1.call-update) | async-done | bytes 3145744 | tf_op jit(solution)/shard_map/all_gather | solution.py:89
  420.9 4.6 broadcast_multiply_fusion
  428.4 1.6 copy.52
  429.9 2.4 slice.162
  432.3 2.5 copy.54
  434.8 1.8 fusion.2
  436.6 1.9 copy-done.1
  439.7 11.7 %cholesky.214 = f32[128,128]{1,0:T(8,128)S(1)} custom-call(f32[128,128]{1,0:T(8,128)S(1)} %cholesky.346), custom_call_target="Cholesky" | custom-call | tf_op jit(solution)/shard_map/jit(cholesky)/cholesky | solution.py:37
  451.4 9.8 %custom-call.29 = f32[1,128,128]{1,2,0:T(8,128)S(1)} custom-call(f32[1,128,128]{2,1,0:T(8,128)S(1)} %get-tuple-element.116), custom_call_target="InvertDiagBlocksLowerTriangular" | custom-call | tf_op jit(solution)/shard_map/jit(cholesky)/cholesky | solution.py:37
  461.8 11.9 %cholesky.231 = f32[128,128]{1,0:T(8,128)S(1)} custom-call(f32[128,128]{1,0:T(8,128)S(1)} %convolution_subtract_fusion.12), custom_call_target="Cholesky" | custom-call | tf_op jit(solution)/shard_map/jit(cholesky)/cholesky | solution.py:37
  475.9 4.1 while.11
  476.6 1.4 bitcast_dynamic-update-slice_fusion.8
  478.6 1.4 bitcast_dynamic-update-slice_fusion.8
  480.1 19.7 %custom-call.30 = f32[2,128,128]{1,2,0:T(8,128)S(1)} custom-call(f32[2,128,128]{2,1,0:T(8,128)S(1)} %get-tuple-element.54), custom_call_target="InvertDiagBlocksLowerTriangular" | custom-call | tf_op jit(solution)/shard_map/triangular_solve/custom-call.0 | solution.py:51
  499.7 1.7 fusion.6
  501.4 1.5 convolution_subtract_fusion.1
  504.4 1.3 fusion.14
  505.7 1.3 fusion.11
  507.0 2.2 slice_subtract_fusion
  509.9 1.8 copy.58
  514.0 13.2 %cholesky.248 = f32[128,128]{1,0:T(8,128)} custom-call(f32[128,128]{1,0:T(8,128)} %cholesky.349), custom_call_target="Cholesky" | custom-call | tf_op jit(solution)/shard_map/jit(cholesky)/cholesky | solution.py:37
  527.2 1.5 select_reduce_fusion.5
  528.7 1.6 cholesky.273
  530.2 11.3 %custom-call.31 = f32[1,128,128]{1,2,0:T(8,128)} custom-call(f32[1,128,128]{2,1,0:T(8,128)} %get-tuple-element.112), custom_call_target="InvertDiagBlocksLowerTriangular" | custom-call | tf_op jit(solution)/shard_map/jit(cholesky)/cholesky | solution.py:37
  541.5 1.7 constant_dynamic-update-slice_fusion.4
  543.2 1.7 convolution_subtract_fusion.11
  544.9 25.7 %cholesky.265 = f32[128,128]{1,0:T(8,128)} custom-call(f32[128,128]{1,0:T(8,128)} %convolution_subtract_fusion.11), custom_call_target="Cholesky" | custom-call | tf_op jit(solution)/shard_map/jit(cholesky)/cholesky | solution.py:37
  570.7 1.5 select_reduce_fusion.4
  574.7 1.7 select_select_fusion.2
  577.1 7.0 while.12
  577.7 2.9 bitcast_dynamic-update-slice_fusion.9
  581.3 2.8 bitcast_dynamic-update-slice_fusion.9
  584.1 21.1 %custom-call.32 = f32[2,128,128]{1,2,0:T(8,128)} custom-call(f32[2,128,128]{2,1,0:T(8,128)} %get-tuple-element.55), custom_call_target="InvertDiagBlocksLowerTriangular" | custom-call | tf_op jit(solution)/shard_map/triangular_solve/custom-call.0 | solution.py:51
  605.2 1.8 fusion.39
  607.0 1.2 fusion.19
  608.2 2.2 fusion.17
  610.4 1.3 convolution_subtract_fusion.3
  611.7 1.2 fusion.59
  613.0 2.0 convolution_subtract_fusion
  617.2 11.7 %cholesky.282 = f32[128,128]{1,0:T(8,128)S(1)} custom-call(f32[128,128]{1,0:T(8,128)S(1)} %cholesky.352), custom_call_target="Cholesky" | custom-call | tf_op jit(solution)/shard_map/jit(cholesky)/cholesky | solution.py:37
  629.0 9.8 %custom-call.33 = f32[1,128,128]{1,2,0:T(8,128)S(1)} custom-call(f32[1,128,128]{2,1,0:T(8,128)S(1)} %get-tuple-element.108), custom_call_target="InvertDiagBlocksLowerTriangular" | custom-call | tf_op jit(solution)/shard_map/jit(cholesky)/cholesky | solution.py:37
  639.3 12.1 %cholesky.299 = f32[128,128]{1,0:T(8,128)S(1)} custom-call(f32[128,128]{1,0:T(8,128)S(1)} %convolution_subtract_fusion.10), custom_call_target="Cholesky" | custom-call | tf_op jit(solution)/shard_map/jit(cholesky)/cholesky | solution.py:37
  653.9 3.9 while.13
  654.6 1.3 bitcast_dynamic-update-slice_fusion.10
  656.6 1.3 bitcast_dynamic-update-slice_fusion.10
  657.8 19.7 %custom-call.34 = f32[2,128,128]{1,2,0:T(8,128)S(1)} custom-call(f32[2,128,128]{2,1,0:T(8,128)S(1)} %get-tuple-element.56), custom_call_target="InvertDiagBlocksLowerTriangular" | custom-call | tf_op jit(solution)/shard_map/triangular_solve/custom-call.0 | solution.py:51
  681.2 1.3 fusion.32
  685.7 1.5 convolution_subtract_fusion.2
  689.7 11.7 %cholesky.316 = f32[128,128]{1,0:T(8,128)S(1)} custom-call(f32[128,128]{1,0:T(8,128)S(1)} %cholesky.355), custom_call_target="Cholesky" | custom-call | tf_op jit(solution)/shard_map/jit(cholesky)/cholesky | solution.py:37
  701.5 10.0 %custom-call.35 = f32[1,128,128]{1,2,0:T(8,128)S(1)} custom-call(f32[1,128,128]{2,1,0:T(8,128)S(1)} %get-tuple-element.104), custom_call_target="InvertDiagBlocksLowerTriangular" | custom-call | tf_op jit(solution)/shard_map/jit(cholesky)/cholesky | solution.py:37
  713.6 11.7 %cholesky.333 = f32[128,128]{1,0:T(8,128)S(1)} custom-call(f32[128,128]{1,0:T(8,128)S(1)} %convolution_subtract_fusion.9), custom_call_target="Cholesky" | custom-call | tf_op jit(solution)/shard_map/jit(cholesky)/cholesky | solution.py:37
  728.1 4.0 while.14
  728.7 1.4 bitcast_dynamic-update-slice_fusion.11
  730.6 1.4 bitcast_dynamic-update-slice_fusion.11
  732.0 19.7 %custom-call.36 = f32[2,128,128]{1,2,0:T(8,128)S(1)} custom-call(f32[2,128,128]{2,1,0:T(8,128)S(1)} %get-tuple-element.57), custom_call_target="InvertDiagBlocksLowerTriangular" | custom-call | tf_op jit(solution)/shard_map/triangular_solve/custom-call.0 | solution.py:51
  755.5 9.6 %fusion.1 = f32[1024,1024]{1,0:T(8,128)S(1)} fusion(f32[256,256]{1,0:T(8,128)} %pad_maximum_fusion.5, f32[128,256]{1,0:T(8,128)S(1)} %fusion.44, f32[128,256]{1,0:T(8,128)S(1)} %fusion.35, f32[256,256]{1,0:T(8,128)S(1)} %convolution_negate_fusion, f32[256,256]{1,0:T(8,128)S(1)} %convolution_negate_fusion.1, f32[256,256]{1,0:T(8,128)S(1)} %convolution_negate_fusion.2, ...), kind=kLoop, calls=%fused_computation.10 | loop fusion | flops 16777216 | bytes 7602176 | tf_op jit(solution)/shard_map/concatenate | solution.py:73
  765.1 3.6 convolution_bitcast_fusion.3
  768.6 2.1 fusion.97
  770.7 6.7 fusion.3
  (143 shorter events, 40.3 us)
Async XLA Ops:
  7.2 294.3 %all-reduce.5.cloned.1.call-start = ((), (), s32[]{:S(2)}) async-start(), calls=%async_computation.1 | async-start | bytes 6291456
  12.1 291.7 %copy-start.3 = (bf16[256,1024]{1,0:T(8,128)(2,1)S(1)}, bf16[256,1024]{1,0:T(8,128)(2,1)}, u32[]{:S(2)}) copy-start(bf16[256,1024]{1,0:T(8,128)(2,1)} %param.5) | copy-start | bytes 1572868
  14.1 406.9 %all-gather.3.cloned.1.call-start = ((), (), s32[]{:S(2)}) async-start(), calls=%async_computation | async-start | bytes 3151872 | tf_op jit(solution)/shard_map/all_gather | solution.py:89
  303.9 199.9 %copy-start.5 = (f32[256,256]{1,0:T(8,128)}, f32[256,256]{1,0:T(8,128)S(1)}, u32[]{:S(2)}) copy-start(f32[256,256]{1,0:T(8,128)S(1)} %fusion.25) | copy-start | bytes 786436
  436.6 1.9 copy-start.1
  499.7 7.2 copy-start.2
  504.4 1.3 copy-start.9
  507.0 98.2 %copy-start.6 = (f32[256,256]{1,0:T(8,128)S(1)}, f32[256,256]{1,0:T(8,128)}, u32[]{:S(2)}) copy-start(f32[256,256]{1,0:T(8,128)} %copy-done.5) | copy-start | bytes 786436
  512.7 0.7 copy-start.16
  610.4 67.1 %copy-start.7 = (f32[256,256]{1,0:T(8,128)S(1)}, f32[256,256]{1,0:T(8,128)}, u32[]{:S(2)}) copy-start(f32[256,256]{1,0:T(8,128)} %copy-done.5) | copy-start | bytes 786436
  615.0 65.3 %copy-start.17 = (f32[2,128,128]{1,2,0:T(8,128)S(1)}, f32[2,128,128]{1,2,0:T(8,128)}, u32[]{:S(2)}) copy-start(f32[2,128,128]{1,2,0:T(8,128)} %custom-call.32) | copy-start | bytes 393220
  615.0 65.6 %copy-start.8 = (f32[128,256]{1,0:T(8,128)S(1)}, f32[128,256]{1,0:T(8,128)}, u32[]{:S(2)}) copy-start(f32[128,256]{1,0:T(8,128)} %fusion.39) | copy-start | bytes 393220
  615.0 67.5 %copy-start.10 = (f32[128,256]{1,0:T(8,128)S(1)}, f32[128,256]{1,0:T(8,128)}, u32[]{:S(2)}) copy-start(f32[128,256]{1,0:T(8,128)} %copy-done.9) | copy-start | bytes 393220
  616.0 67.2 %copy-start.12 = (f32[256,256]{1,0:T(8,128)S(1)}, f32[256,256]{1,0:T(8,128)}, u32[]{:S(2)}) copy-start(f32[256,256]{1,0:T(8,128)} %fusion.11) | copy-start | bytes 786436
  657.8 30.1 %copy-start.11 = (f32[256,256]{1,0:T(8,128)S(1)}, f32[256,256]{1,0:T(8,128)}, u32[]{:S(2)}) copy-start(f32[256,256]{1,0:T(8,128)} %fusion.14) | copy-start | bytes 786436
  680.6 8.3 %copy-start.13 = (f32[256,256]{1,0:T(8,128)S(1)}, f32[256,256]{1,0:T(8,128)}, u32[]{:S(2)}) copy-start(f32[256,256]{1,0:T(8,128)} %fusion.17) | copy-start | bytes 786436
  689.5 64.5 %copy-start.14 = (f32[256,256]{1,0:T(8,128)S(1)}, f32[256,256]{1,0:T(8,128)}, u32[]{:S(2)}) copy-start(f32[256,256]{1,0:T(8,128)} %fusion.32) | copy-start | bytes 786436
  689.7 11.7 %copy-start.15 = (f32[256,256]{1,0:T(8,128)}, f32[256,256]{1,0:T(8,128)S(1)}, u32[]{:S(2)}) copy-start(f32[256,256]{1,0:T(8,128)S(1)} %fusion.21) | copy-start | bytes 786436
  765.0 3.6 copy-start
  765.0 5.7 copy-start.4
Sparse Core Ops, SparseCore 0:
  14.2 287.2 all-reduce.4
  307.0 113.9 all-gather.2
where the time goes:
time: 790 us; the launch traced here: 785 us
  waiting for transfers between devices  404 us (51%)
  other arithmetic  263 us (33%)
  matrix products  56.8 us (7%)
  local copies, waits for them, and re-layouts  40 us (5%)
  between operations  21 us (3%)
    unnamed x3, waiting for transfers between devices  287 us
    another operation x27, other arithmetic, blocked_inverse_factor(): diagonal = jnp.linalg.cholesky(trailing[:block_size, :block_size])  159 us
    all_gather x1, waiting for transfers between devices, per_device(): summed = lax.all_gather(shares, ('rows', 'sub'), axis=0, tiled=True)  117 us
    another operation x10, other arithmetic, blocked_inverse_factor(): lax.linalg.triangular_solve(factor_blocks[index][index], eye_block, left_...  82.6 us
    another operation x29, local copies, waits for them, and re-layouts, blocked_inverse_factor(): lax.linalg.triangular_solve(factor_blocks[index][index], eye_block, left_...  19.6 us
    dot_general x19, matrix products, exact_dot(): return jnp.dot(left, right, precision=lax.Precision.HIGHEST)  17.8 us
  transfers between devices with their start and end apart: 2, of which 2 were waited for; matrix products, arithmetic and copies ran while one was open for 0% of the time, Pallas kernels for 0%

commit v1 on v0

v1 whole, which is shorter than its diff:
```python
import jax
import jax.numpy as jnp
from jax import lax
from jax.experimental import pallas as pl
from jax.experimental.pallas import tpu as pltpu
from jax.sharding import Mesh
from jax.sharding import PartitionSpec as P

WIDTH = 1024
BLOCK = 128
COUNT = WIDTH // BLOCK
PAIRS = COUNT * (COUNT + 1) // 2
HALF = PAIRS // 2
HALF_ROWS = HALF * BLOCK
BASE = 32


def qdwh_weights(lower_bound):
    value = lower_bound[0]
    square = value * value
    delta = jnp.cbrt(4.0 * (1.0 - square) / (square * square))
    root = jnp.sqrt(1.0 + delta)
    alpha = root + 0.5 * jnp.sqrt(8.0 - 4.0 * delta + 8.0 * (2.0 - square) / (square * root))
    beta = (alpha - 1.0) ** 2 / 4.0
    shift = alpha + beta - 1.0
    return (beta / shift, alpha - beta / shift, shift)


def iota(shape, dimension):
    return lax.broadcasted_iota(jnp.int32, shape, dimension)


def dot_nn(left, right):
    return jnp.dot(left, right, preferred_element_type=jnp.float32)


def dot_nt(left, right):
    return lax.dot_general(
        left, right, (((1,), (1,)), ((), ())), preferred_element_type=jnp.float32
    )


def dot_tn(left, right):
    return lax.dot_general(
        left, right, (((0,), (0,)), ((), ())), preferred_element_type=jnp.float32
    )


def split(value):
    high = value.astype(jnp.bfloat16)
    rest = value - high.astype(jnp.float32)
    middle = rest.astype(jnp.bfloat16)
    low = (rest - middle.astype(jnp.float32)).astype(jnp.bfloat16)
    return high, middle, low


def left_terms(value, axis):
    high, middle, low = split(value)
    return jnp.concatenate([high, high, middle, high, low, middle], axis=axis)


def right_terms(value, axis):
    high, middle, low = split(value)
    return jnp.concatenate([high, middle, high, low, high, middle], axis=axis)


def block_pairs():
    return [(row, column) for row in range(COUNT) for column in range(row, COUNT)]


def gram_kernel(slab_ref, mine_ref, other_ref):
    core = lax.axis_index("core")
    for side in range(2):

        @pl.when(core == side)
        def _():
            position = 0
            for row in range(COUNT):
                product = dot_tn(
                    slab_ref[:, row * BLOCK : (row + 1) * BLOCK], slab_ref[:, row * BLOCK :]
                )
                for step in range(COUNT - row):
                    half, place = divmod(position, HALF)
                    target = mine_ref if half == side else other_ref
                    target[place * BLOCK : (place + 1) * BLOCK, :] = product[
                        :, step * BLOCK : (step + 1) * BLOCK
                    ]
                    position += 1


def gram_blocks(slab):
    shape = jax.ShapeDtypeStruct((HALF_ROWS, BLOCK), jnp.float32)
    return pl.pallas_call(
        gram_kernel,
        out_shape=(shape, shape),
        in_specs=[pl.BlockSpec(memory_space=pltpu.VMEM)],
        out_specs=(pl.BlockSpec(memory_space=pltpu.VMEM),) * 2,
        compiler_params=pltpu.CompilerParams(vmem_limit_bytes=32 * 2**20),
    )(slab)


def eliminate(row, offset):
    groups = BASE // 8
    lane = iota((8, BLOCK), 1)
    sub = iota((8, BLOCK), 0)
    columns = []
    for column in range(BASE):
        columns.append(
            [
                None
                if group < column // 8
                else jnp.broadcast_to(
                    row[8 * group : 8 * group + 8, offset + column : offset + column + 1],
                    (8, BLOCK),
                )
                for group in range(groups)
            ]
        )
    result = []
    for group in range(groups):
        eye = jnp.where(lane == sub + (offset + 8 * group), 1.0, 0.0)
        inside = (lane >= offset) & (lane < offset + BASE)
        result.append(jnp.where(inside, eye, row[8 * group : 8 * group + 8]))
    pivots = [jnp.ones((8, BLOCK), jnp.float32) for _ in range(groups)]

    def spread(value, sublane):
        return jnp.broadcast_to(value[sublane : sublane + 1], (8, BLOCK))

    for column in range(BASE):
        home, sublane = divmod(column, 8)
        current = columns[column]
        pivot = spread(current[home], sublane)
        inverse_pivot = 1.0 / pivot
        pivots[home] = jnp.where(sub == sublane, pivot, pivots[home])
        scaled = [None] * groups
        for group in range(home, groups):
            scaled[group] = current[group] * inverse_pivot
        for later in range(column + 1, BASE):
            factor = spread(current[later // 8], later % 8)
            for group in range(later // 8, groups):
                columns[later][group] = columns[later][group] - scaled[group] * factor
        source = spread(result[home], sublane)
        for group in range(home, groups):
            multiplier = scaled[group]
            if group == home:
                if sublane == 7:
                    continue
                multiplier = jnp.where(sub > sublane, multiplier, 0.0)
            result[group] = result[group] - multiplier * source
    return jnp.concatenate(
        [result[group] * lax.rsqrt(pivots[group]) for group in range(groups)], axis=0
    )


def inverse_factor_block(block):
    count = BLOCK // BASE
    rows = [block[BASE * index : BASE * (index + 1)] for index in range(count)]
    lane = iota((BASE, BLOCK), 1)
    out = []
    for index in range(count):
        start = BASE * index
        done = eliminate(rows[index], start)
        out.append(jnp.where(lane < start + BASE, done, 0.0))
        if index + 1 < count:
            update = dot_tn(left_terms(done, 0), right_terms(done, 0))
            for later in range(index + 1, count):
                kept = jnp.where((lane >= start) & (lane < start + BASE), 0.0, rows[later])
                rows[later] = kept - update[BASE * later : BASE * (later + 1)]
    return jnp.concatenate(out, axis=0)


def step_kernel(
    weights_ref, mine_ref, other_ref, slab_ref, out_ref, check_ref,
    matrix, panel, terms, solved, checksum, checked,
):
    core = lax.axis_index("core")
    first, second, scale = weights_ref[0], weights_ref[1], weights_ref[2]
    diagonal = jnp.where(iota((BLOCK, BLOCK), 0) == iota((BLOCK, BLOCK), 1), 1.0, 0.0)
    matrix[...] = jnp.zeros_like(matrix)
    for side in range(2):

        @pl.when(core == side)
        def _():
            for position, (row, column) in enumerate(block_pairs()):
                half, place = divmod(position, HALF)
                source = mine_ref if half == side else other_ref
                value = source[place * BLOCK : (place + 1) * BLOCK, :] * scale
                if row == column:
                    value = value + diagonal
                matrix[
                    row * BLOCK : (row + 1) * BLOCK, column * BLOCK : (column + 1) * BLOCK
                ] = value

    column_block = iota((BLOCK, WIDTH), 1) // BLOCK
    rows_dev = slab_ref.shape[0]
    checksum[...] = jnp.broadcast_to(
        jnp.sum(slab_ref[...].astype(jnp.float32), axis=0, keepdims=True) / (rows_dev**0.5),
        checksum.shape,
    )
    checked[...] = jnp.zeros_like(checked)
    solved[...] = jnp.zeros_like(solved)

    def step(index, carry):
        here = pl.ds(pl.multiple_of(index * BLOCK, BLOCK), BLOCK)
        inverse_block = inverse_factor_block(matrix[here, here])
        panel[...] = dot_nn(left_terms(inverse_block, 1), right_terms(matrix[here, :], 0))
        panel[:, here] = inverse_block
        value = panel[...]
        terms[...] = right_terms(value, 0)

        def update(later, carry):
            there = pl.ds(pl.multiple_of(later * BLOCK, BLOCK), BLOCK)
            left = left_terms(panel[:, there].T, 1)
            kept = jnp.where(column_block == index, 0.0, matrix[there, :])
            matrix[there, :] = kept - dot_nn(left, terms[...])
            return carry

        lax.fori_loop(index + 1, COUNT, update, 0)
        inverse = jnp.where(column_block <= index, value, 0.0)
        inverse_half = inverse.astype(jnp.bfloat16)
        projected = dot_nt(slab_ref[...], inverse_half).astype(jnp.bfloat16)
        solved[...] += dot_nn(projected, inverse_half)
        weight = jnp.sum(inverse * checksum[0:1, :], axis=1, keepdims=True)
        checked[...] += (inverse * weight).reshape(BLOCK // 8, 8, WIDTH).sum(axis=0)
        return carry

    lax.fori_loop(0, COUNT, step, 0)
    out_ref[...] = first * slab_ref[...].astype(jnp.float32) + second * solved[...]
    check_ref[...] = first * checksum[0:1, :] + second * jnp.sum(
        checked[...], axis=0, keepdims=True
    )


def polar_step(weights, mine, other, slab):
    rows_dev = slab.shape[0]
    vmem = pl.BlockSpec(memory_space=pltpu.VMEM)
    return pl.pallas_call(
        step_kernel,
        out_shape=(
            jax.ShapeDtypeStruct((rows_dev, WIDTH), jnp.float32),
            jax.ShapeDtypeStruct((1, WIDTH), jnp.float32),
        ),
        in_specs=[pl.BlockSpec(memory_space=pltpu.SMEM), vmem, vmem, vmem],
        out_specs=(vmem, vmem),
        scratch_shapes=[
            pltpu.VMEM((WIDTH, WIDTH), jnp.float32),
            pltpu.VMEM((BLOCK, WIDTH), jnp.float32),
            pltpu.VMEM((6 * BLOCK, WIDTH), jnp.bfloat16),
            pltpu.VMEM((rows_dev, WIDTH), jnp.float32),
            pltpu.VMEM((8, WIDTH), jnp.float32),
            pltpu.VMEM((8, WIDTH), jnp.float32),
        ],
        compiler_params=pltpu.CompilerParams(vmem_limit_bytes=48 * 2**20),
    )(weights, mine, other, slab)


def exchange(parts, axis):
    return lax.all_to_all(parts, axis, 0, 0, tiled=True)


def shared(part, count):
    return jnp.broadcast_to(part[None], (count,) + part.shape)


def swap(value):
    return lax.ppermute(value, "core", [(0, 1), (1, 0)])


def sum_over_devices(mine, other):
    size_x, size_y, size_z = (lax.axis_size(name) for name in ("x", "y", "z"))
    own = mine + swap(other)
    own = exchange(own.reshape(size_x, -1, BLOCK), "x").sum(axis=0)
    own = exchange(own.reshape(size_y, -1, BLOCK), "y").sum(axis=0)
    own = exchange(shared(own, size_z), "z").sum(axis=0)
    own = exchange(shared(own, size_y), "y").reshape(-1, BLOCK)
    own = exchange(shared(own, size_x), "x").reshape(-1, BLOCK)
    return own, swap(own)


def per_device(slab, lower_bound):
    devices_all = 1
    for name in ("y", "x", "z", "core"):
        devices_all *= lax.axis_size(name)
    first, second, shift = qdwh_weights(lower_bound)
    weights = jnp.stack([first, second, shift / (slab.shape[0] * devices_all)])
    mine, other = sum_over_devices(*gram_blocks(slab))
    return polar_step(weights, mine, other, slab)


def solution(mesh):
    names = ("y", "x", "z", "core")
    wide = Mesh(mesh.devices.reshape(8, 4, 8, 2), names)
    return jax.shard_map(
        per_device,
        mesh=wide,
        in_specs=(P(names, None), P()),
        out_specs=(P(names, None), P(names, None)),
        check_vma=False,
    )
```

time: 790 us -> 149 us (0.19)
  waiting for transfers between devices: 404 us -> 3.91 us
  other arithmetic: 263 us -> 0.32 us
  blocking collectives: 0 us -> 76.6 us
  matrix products: 56.8 us -> 0 us
  Pallas kernels: 0 us -> 47.8 us
  local copies, waits for them, and re-layouts: 40 us -> 1.16 us
  between operations: 21 us -> 1.63 us
  starting transfers between devices: 0.08 us -> 17 us
    unnamed x3 -> x0, waiting for transfers between devices: 287 us -> none
    another operation x37 -> x1, other arithmetic: 241 us -> 0.08 us  [per_device(): weights = jnp.stack([first, second, shift / (slab.shape[0] * devices_all)])]
    all_gather x1 -> x0, waiting for transfers between devices: 117 us -> none  [per_device(): summed = lax.all_gather(shares, ('rows', 'sub'), axis=0, tiled=True)]
    all_to_all x0 -> x5, blocking collectives: none -> 76.6 us  [exchange(): return lax.all_to_all(parts, axis, 0, 0, tiled=True)]
    pallas_call x0 -> x2, Pallas kernels: none -> 47.8 us  [the longest x1 47.2 us: polar_step(): pl.pallas_call(step_kernel, out_shape=(jax.ShapeDtypeStruct((rows_dev, WI...]
    dot_general x25 -> x0, matrix products: 34.2 us -> none  [the longest x19 17.8 us: exact_dot(): return jnp.dot(left, right, precision=lax.Precision.HIGHEST)]
    another operation x29 -> x0, matrix products: 22.6 us -> none  [the longest x9 10.1 us: blocked_inverse_factor(): lax.linalg.triangular_solve(diagonal, below, left_side=False, lower=True,...]
    another operation x38 -> x0, local copies, waits for them, and re-layouts: 21.9 us -> none  [the longest x29 19.6 us: blocked_inverse_factor(): lax.linalg.triangular_solve(factor_blocks[index][index], eye_block, left_...]
where the time goes in v1:
time: 149 us; the launch traced here: 148 us
  blocking collectives  76.6 us (51%)
  Pallas kernels  47.8 us (32%)
  starting transfers between devices  17 us (11%)
  waiting for transfers between devices  3.91 us (3%)
  between operations  1.63 us (1%)
    all_to_all x5, blocking collectives, exchange(): return lax.all_to_all(parts, axis, 0, 0, tiled=True)  76.6 us
    pallas_call x1, Pallas kernels, polar_step(): pl.pallas_call(step_kernel, out_shape=(jax.ShapeDtypeStruct((rows_dev, WI...  47.2 us
    ppermute x2, starting transfers between devices, swap(): return lax.ppermute(value, 'core', [(0, 1), (1, 0)])  17 us
    ppermute x2, waiting for transfers between devices, swap(): return lax.ppermute(value, 'core', [(0, 1), (1, 0)])  3.91 us
  transfers between devices with their start and end apart: 2, of which 2 were waited for; matrix products, arithmetic and copies ran while one was open for 0% of the time, Pallas kernels for 0%

profile of v1, /device:TPU:1, one launch (start us, length us, event | category | flops | bytes accessed | tf_op | source)
XLA Modules:
  0.0 148.4 jit_solution(11374612058204001820)
XLA Ops:
  0.6 0.0 copy-start
  0.6 1.0 copy-done
  1.7 0.5 shard_map.41
  2.2 8.8 %collective-permute-start = (f32[2304,128]{1,0:T(8,128)S(1)}, f32[2304,128]{1,0:T(8,128)S(1)}, u32[]{:S(2)}, u32[]{:S(2)}) collective-permute-start(f32[2304,128]{1,0:T(8,128)S(1)} %get-tuple-element.5), channel_id=1, source_target_pairs={{0,1},{1,0},{2,3},{3,2},{4,5},{5,4},{6,7},{7,6},{8,9},{9,8},{10,11... | collective-permute-start | bytes 3538952 | tf_op jit(solution)/shard_map/ppermute | solution.py:266
  11.0 2.5 %collective-permute-done = f32[2304,128]{1,0:T(8,128)S(1)} collective-permute-done((f32[2304,128]{1,0:T(8,128)S(1)}, f32[2304,128]{1,0:T(8,128)S(1)}, u32[]{:S(2)}, u32[]{:S(2)}) %collective-permute-start) | collective-permute-done | bytes 1179680 | tf_op jit(solution)/shard_map/ppermute | solution.py:266
  13.5 0.1 add.21
  13.6 18.7 %all_to_all.25 = f32[4,576,128]{2,1,0:T(8,128)S(1)} all-to-all(f32[4,576,128]{2,1,0:T(8,128)S(1)} %bitcast.10), channel_id=1, replica_groups=mesh['y'=8,'x'=4,'z'=8,'core'=2] {'x'}, dimensions={0} | all-to-all | bytes 2359296 | tf_op jit(solution)/shard_map/all_to_all | solution.py:258
  32.3 0.1 reduce_sum.27
  32.4 12.6 %all_to_all.26 = f32[8,72,128]{2,1,0:T(8,128)S(1)} all-to-all(f32[8,72,128]{2,1,0:T(8,128)S(1)} %bitcast.11), channel_id=1, replica_groups=mesh['y'=8,'x'=4,'z'=8,'core'=2] {'y'}, dimensions={0} | all-to-all | bytes 589824 | tf_op jit(solution)/shard_map/all_to_all | solution.py:258
  45.0 18.3 %all_to_all.27 = f32[8,72,128]{2,1,0:T(8,128)S(1)} all-to-all(f32[8,72,128]{2,1,0:T(8,128)S(1)} %broadcast_in_dim.8), channel_id=1, replica_groups=mesh['y'=8,'x'=4,'z'=8,'core'=2] {'z'}, dimensions={0} | all-to-all | bytes 589824 | tf_op jit(solution)/shard_map/all_to_all | solution.py:258
  63.3 13.4 %all_to_all.28 = f32[8,72,128]{2,1,0:T(8,128)S(1)} all-to-all(f32[8,72,128]{2,1,0:T(8,128)S(1)} %broadcast_in_dim.9), channel_id=1, replica_groups=mesh['y'=8,'x'=4,'z'=8,'core'=2] {'y'}, dimensions={0} | all-to-all | bytes 589824 | tf_op jit(solution)/shard_map/all_to_all | solution.py:258
  76.7 0.1 broadcast_in_dim.22
  76.8 0.0 copy-start.1
  76.8 13.7 %all_to_all.29 = f32[4,576,128]{2,1,0:T(8,128)S(1)} all-to-all(f32[4,576,128]{2,1,0:T(8,128)S(1)} %broadcast_in_dim.22), channel_id=1, replica_groups=mesh['y'=8,'x'=4,'z'=8,'core'=2] {'x'}, dimensions={0} | all-to-all | bytes 2359296 | tf_op jit(solution)/shard_map/all_to_all | solution.py:258
  90.5 8.3 %collective-permute-start.1 = (f32[2304,128]{1,0:T(8,128)S(1)}, f32[2304,128]{1,0:T(8,128)S(1)}, u32[]{:S(2)}, u32[]{:S(2)}) collective-permute-start(f32[2304,128]{1,0:T(8,128)S(1)} %bitcast.8), channel_id=1, source_target_pairs={{0,1},{1,0},{2,3},{3,2},{4,5},{5,4},{6,7},{7,6},{8,9},{9,8},{10,11... | collective-permute-start | bytes 3538952 | tf_op jit(solution)/shard_map/ppermute | solution.py:266
  99.7 0.1 pad_maximum_fusion.weights_ref
  99.7 1.5 collective-permute-done.1.other_ref
  101.2 0.0 copy-done.1
  101.2 47.2 %shard_map.42 = (f32[256,1024]{1,0:T(8,128)}, f32[1,1024]{1,0:T(1,128)}) custom-call(f32[3]{0:T(128)S(1)} %pad_maximum_fusion.weights_ref, f32[2304,128]{1,0:T(8,128)S(1)} %bitcast.9, f32[2304,128]{1,0:T(8,128)S(1)} %collective-permute-done.1.other_ref, bf16[256,1024]{1,0:T(8,128)(2,1)S(1)} %copy-done.1), custom_call_target="tpu_custom_call" | custom-call | tf_op jit(solution)/shard_map/pallas_call | solution.py:237
  (4 shorter events, 0.1 us)
Async XLA Ops:
  0.6 1.0 copy-start
  2.2 11.3 %collective-permute-start = (f32[2304,128]{1,0:T(8,128)S(1)}, f32[2304,128]{1,0:T(8,128)S(1)}, u32[]{:S(2)}, u32[]{:S(2)}) collective-permute-start(f32[2304,128]{1,0:T(8,128)S(1)} %get-tuple-element.5), channel_id=1, source_target_pairs={{0,1},{1,0},{2,3},{3,2},{4,5},{5,4},{6,7},{7,6},{8,9},{9,8},{10,11... | collective-permute-start | bytes 3538952 | tf_op jit(solution)/shard_map/ppermute | solution.py:266
  76.8 24.4 %copy-start.1 = (bf16[256,1024]{1,0:T(8,128)(2,1)S(1)}, bf16[256,1024]{1,0:T(8,128)(2,1)}, u32[]{:S(2)}) copy-start(bf16[256,1024]{1,0:T(8,128)(2,1)} %slab_ref.3) | copy-start | bytes 1572868
  90.5 10.7 %collective-permute-start.1 = (f32[2304,128]{1,0:T(8,128)S(1)}, f32[2304,128]{1,0:T(8,128)S(1)}, u32[]{:S(2)}, u32[]{:S(2)}) collective-permute-start(f32[2304,128]{1,0:T(8,128)S(1)} %bitcast.8), channel_id=1, source_target_pairs={{0,1},{1,0},{2,3},{3,2},{4,5},{5,4},{6,7},{7,6},{8,9},{9,8},{10,11... | collective-permute-start | bytes 3538952 | tf_op jit(solution)/shard_map/ppermute | solution.py:266

commit v2 on v1

--- a/solution.py
+++ b/solution.py
@@ -13,6 +13,7 @@
 HALF = PAIRS // 2
 HALF_ROWS = HALF * BLOCK
 BASE = 32
+AXES = ("y_high", "y_low", "x", "z_high", "z_low", "core")
 
 
 def qdwh_weights(lower_bound):
@@ -267,19 +268,21 @@
 
 
 def sum_over_devices(mine, other):
-    size_x, size_y, size_z = (lax.axis_size(name) for name in ("x", "y", "z"))
+    near = ("x", "y_low", "z_low")
+    count = 1
+    for name in near:
+        count *= lax.axis_size(name)
     own = mine + swap(other)
-    own = exchange(own.reshape(size_x, -1, BLOCK), "x").sum(axis=0)
-    own = exchange(own.reshape(size_y, -1, BLOCK), "y").sum(axis=0)
-    own = exchange(shared(own, size_z), "z").sum(axis=0)
-    own = exchange(shared(own, size_y), "y").reshape(-1, BLOCK)
-    own = exchange(shared(own, size_x), "x").reshape(-1, BLOCK)
+    own = exchange(own.reshape(count, -1, BLOCK), near).sum(axis=0)
+    for name in ("y_high", "z_high"):
+        own = exchange(shared(own, lax.axis_size(name)), name).sum(axis=0)
+    own = exchange(shared(own, count), near).reshape(-1, BLOCK)
     return own, swap(own)
 
 
 def per_device(slab, lower_bound):
     devices_all = 1
-    for name in ("y", "x", "z", "core"):
+    for name in AXES:
         devices_all *= lax.axis_size(name)
     first, second, shift = qdwh_weights(lower_bound)
     weights = jnp.stack([first, second, shift / (slab.shape[0] * devices_all)])
@@ -288,12 +291,11 @@
 
 
 def solution(mesh):
-    names = ("y", "x", "z", "core")
-    wide = Mesh(mesh.devices.reshape(8, 4, 8, 2), names)
+    wide = Mesh(mesh.devices.reshape(4, 2, 4, 4, 2, 2), AXES)
     return jax.shard_map(
         per_device,
         mesh=wide,
-        in_specs=(P(names, None), P()),
-        out_specs=(P(names, None), P(names, None)),
+        in_specs=(P(AXES, None), P()),
+        out_specs=(P(AXES, None), P(AXES, None)),
         check_vma=False,
     )

time: 149 us -> 139 us (0.933)
  blocking collectives: 76.6 us -> 66.5 us
    all_to_all x5 -> x4, blocking collectives: 76.6 us -> 66.5 us  [exchange(): return lax.all_to_all(parts, axis, 0, 0, tiled=True)]
where the time goes in v2:
time: 139 us
  blocking collectives  66.5 us (48%)
  Pallas kernels  47.9 us (34%)
  starting transfers between devices  17.3 us (12%)
  waiting for transfers between devices  3.91 us (3%)
  between operations  1.63 us (1%)
    all_to_all x4, blocking collectives, exchange(): return lax.all_to_all(parts, axis, 0, 0, tiled=True)  66.5 us
    pallas_call x1, Pallas kernels, polar_step(): pl.pallas_call(step_kernel, out_shape=(jax.ShapeDtypeStruct((rows_dev, WI...  47.3 us
    ppermute x2, starting transfers between devices, swap(): return lax.ppermute(value, 'core', [(0, 1), (1, 0)])  17.3 us
    ppermute x2, waiting for transfers between devices, swap(): return lax.ppermute(value, 'core', [(0, 1), (1, 0)])  3.91 us
  transfers between devices with their start and end apart: 2, of which 2 were waited for; matrix products, arithmetic and copies ran while one was open for 0% of the time, Pallas kernels for 0%

profile of v2, /device:TPU:1, one launch (start us, length us, event | category | flops | bytes accessed | tf_op | source)
XLA Modules:
  0.0 138.6 jit_solution(5143563860504493429)
XLA Ops:
  0.6 0.0 copy-start
  0.6 1.0 copy-done
  1.7 0.5 shard_map.41
  2.2 8.8 %collective-permute-start = (f32[2304,128]{1,0:T(8,128)S(1)}, f32[2304,128]{1,0:T(8,128)S(1)}, u32[]{:S(2)}, u32[]{:S(2)}) collective-permute-start(f32[2304,128]{1,0:T(8,128)S(1)} %get-tuple-element.5), channel_id=1, source_target_pairs={{0,1},{1,0},{2,3},{3,2},{4,5},{5,4},{6,7},{7,6},{8,9},{9,8},{10,11... | collective-permute-start | bytes 3538952 | tf_op jit(solution)/shard_map/ppermute | solution.py:267
  11.0 2.5 %collective-permute-done = f32[2304,128]{1,0:T(8,128)S(1)} collective-permute-done((f32[2304,128]{1,0:T(8,128)S(1)}, f32[2304,128]{1,0:T(8,128)S(1)}, u32[]{:S(2)}, u32[]{:S(2)}) %collective-permute-start) | collective-permute-done | bytes 1179680 | tf_op jit(solution)/shard_map/ppermute | solution.py:267
  13.5 0.1 add.21
  13.6 19.8 %all_to_all.20 = f32[16,144,128]{2,1,0:T(8,128)S(1)} all-to-all(f32[16,144,128]{2,1,0:T(8,128)S(1)} %bitcast.8), channel_id=1, replica_groups=mesh['y_high'=4,'y_low'=2,'x'=4,'z_high'=4,'z_low'=2,'core'=2] {'x','y_l..., dimensions={0} | all-to-all | bytes 2359296 | tf_op jit(solution)/shard_map/all_to_all | solution.py:259
  33.4 0.1 reduce_sum.27
  33.5 12.7 %all_to_all.21 = f32[4,144,128]{2,1,0:T(8,128)S(1)} all-to-all(f32[4,144,128]{2,1,0:T(8,128)S(1)} %broadcast_in_dim.6), channel_id=1, replica_groups=mesh['y_high'=4,'y_low'=2,'x'=4,'z_high'=4,'z_low'=2,'core'=2] {'y_high'}, dimensions={0} | all-to-all | bytes 589824 | tf_op jit(solution)/shard_map/all_to_all | solution.py:259
  46.2 18.6 %all_to_all.22 = f32[4,144,128]{2,1,0:T(8,128)S(1)} all-to-all(f32[4,144,128]{2,1,0:T(8,128)S(1)} %broadcast_in_dim.7), channel_id=1, replica_groups=mesh['y_high'=4,'y_low'=2,'x'=4,'z_high'=4,'z_low'=2,'core'=2] {'z_high'}, dimensions={0} | all-to-all | bytes 589824 | tf_op jit(solution)/shard_map/all_to_all | solution.py:259
  64.9 0.1 broadcast_in_dim.8
  65.0 0.0 copy-start.1
  65.0 15.4 %all_to_all.23 = f32[16,144,128]{2,1,0:T(8,128)S(1)} all-to-all(f32[16,144,128]{2,1,0:T(8,128)S(1)} %broadcast_in_dim.8), channel_id=1, replica_groups=mesh['y_high'=4,'y_low'=2,'x'=4,'z_high'=4,'z_low'=2,'core'=2] {'x','y_l..., dimensions={0} | all-to-all | bytes 2359296 | tf_op jit(solution)/shard_map/all_to_all | solution.py:259
  80.4 8.5 %collective-permute-start.1 = (f32[2304,128]{1,0:T(8,128)S(1)}, f32[2304,128]{1,0:T(8,128)S(1)}, u32[]{:S(2)}, u32[]{:S(2)}) collective-permute-start(f32[2304,128]{1,0:T(8,128)S(1)} %bitcast.6), channel_id=1, source_target_pairs={{0,1},{1,0},{2,3},{3,2},{4,5},{5,4},{6,7},{7,6},{8,9},{9,8},{10,11... | collective-permute-start | bytes 3538952 | tf_op jit(solution)/shard_map/ppermute | solution.py:267
  89.8 0.1 pad_maximum_fusion.weights_ref
  89.8 1.5 %collective-permute-done.1.other_ref = f32[2304,128]{1,0:T(8,128)S(1)} collective-permute-done((f32[2304,128]{1,0:T(8,128)S(1)}, f32[2304,128]{1,0:T(8,128)S(1)}, u32[]{:S(2)}, u32[]{:S(2)}) %collective-permute-start.1) | collective-permute-done | bytes 1179680 | tf_op jit(solution)/shard_map/ppermute | solution.py:267
  91.3 0.0 copy-done.1
  91.3 47.3 %shard_map.42 = (f32[256,1024]{1,0:T(8,128)}, f32[1,1024]{1,0:T(1,128)}) custom-call(f32[3]{0:T(128)S(1)} %pad_maximum_fusion.weights_ref, f32[2304,128]{1,0:T(8,128)S(1)} %bitcast.7, f32[2304,128]{1,0:T(8,128)S(1)} %collective-permute-done.1.other_ref, bf16[256,1024]{1,0:T(8,128)(2,1)S(1)} %copy-done.1), custom_call_target="tpu_custom_call" | custom-call | tf_op jit(solution)/shard_map/pallas_call | solution.py:238
  (4 shorter events, 0.1 us)
Async XLA Ops:
  0.6 1.0 copy-start
  2.2 11.3 %collective-permute-start = (f32[2304,128]{1,0:T(8,128)S(1)}, f32[2304,128]{1,0:T(8,128)S(1)}, u32[]{:S(2)}, u32[]{:S(2)}) collective-permute-start(f32[2304,128]{1,0:T(8,128)S(1)} %get-tuple-element.5), channel_id=1, source_target_pairs={{0,1},{1,0},{2,3},{3,2},{4,5},{5,4},{6,7},{7,6},{8,9},{9,8},{10,11... | collective-permute-start | bytes 3538952 | tf_op jit(solution)/shard_map/ppermute | solution.py:267
  65.0 26.3 %copy-start.1 = (bf16[256,1024]{1,0:T(8,128)(2,1)S(1)}, bf16[256,1024]{1,0:T(8,128)(2,1)}, u32[]{:S(2)}) copy-start(bf16[256,1024]{1,0:T(8,128)(2,1)} %slab_ref.3) | copy-start | bytes 1572868
  80.4 10.9 %collective-permute-start.1 = (f32[2304,128]{1,0:T(8,128)S(1)}, f32[2304,128]{1,0:T(8,128)S(1)}, u32[]{:S(2)}, u32[]{:S(2)}) collective-permute-start(f32[2304,128]{1,0:T(8,128)S(1)} %bitcast.6), channel_id=1, source_target_pairs={{0,1},{1,0},{2,3},{3,2},{4,5},{5,4},{6,7},{7,6},{8,9},{9,8},{10,11... | collective-permute-start | bytes 3538952 | tf_op jit(solution)/shard_map/ppermute | solution.py:267

commit v3 on v2

v3 whole, which is shorter than its diff:
```python
import jax
import jax.numpy as jnp
from jax import lax
from jax.experimental import pallas as pl
from jax.experimental.pallas import tpu as pltpu
from jax.sharding import Mesh
from jax.sharding import PartitionSpec as P

WIDTH = 1024
BLOCK = 128
COUNT = WIDTH // BLOCK
PAIRS = COUNT * (COUNT + 1) // 2
HALF = PAIRS // 2
HALF_ROWS = HALF * BLOCK
BASE = 64
GROUP = 8
AHEAD = 3
AXES = ("y_high", "y_low", "x", "z_high", "z_low", "core")


def qdwh_weights(lower_bound):
    value = lower_bound[0]
    square = value * value
    delta = jnp.cbrt(4.0 * (1.0 - square) / (square * square))
    root = jnp.sqrt(1.0 + delta)
    alpha = root + 0.5 * jnp.sqrt(8.0 - 4.0 * delta + 8.0 * (2.0 - square) / (square * root))
    beta = (alpha - 1.0) ** 2 / 4.0
    shift = alpha + beta - 1.0
    return (beta / shift, alpha - beta / shift, shift)


def iota(shape, dimension):
    return lax.broadcasted_iota(jnp.int32, shape, dimension)


def dot_nn(left, right):
    return jnp.dot(left, right, preferred_element_type=jnp.float32)


def dot_nt(left, right):
    return lax.dot_general(
        left, right, (((1,), (1,)), ((), ())), preferred_element_type=jnp.float32
    )


def dot_tn(left, right):
    return lax.dot_general(
        left, right, (((0,), (0,)), ((), ())), preferred_element_type=jnp.float32
    )


def split(value):
    high = value.astype(jnp.bfloat16)
    rest = value - high.astype(jnp.float32)
    middle = rest.astype(jnp.bfloat16)
    low = (rest - middle.astype(jnp.float32)).astype(jnp.bfloat16)
    return high, middle, low


def left_terms(parts, axis):
    high, middle, low = parts
    return jnp.concatenate([high, high, middle, high, low, middle], axis=axis)


def right_terms(parts, axis):
    high, middle, low = parts
    return jnp.concatenate([high, middle, high, low, high, middle], axis=axis)


def block_pairs():
    return [(row, column) for row in range(COUNT) for column in range(row, COUNT)]


def gram_kernel(slab_ref, mine_ref, other_ref):
    core = lax.axis_index("core")
    for side in range(2):

        @pl.when(core == side)
        def _():
            position = 0
            for row in range(COUNT):
                product = dot_tn(
                    slab_ref[:, row * BLOCK : (row + 1) * BLOCK], slab_ref[:, row * BLOCK :]
                )
                for step in range(COUNT - row):
                    half, place = divmod(position, HALF)
                    target = mine_ref if half == side else other_ref
                    target[place * BLOCK : (place + 1) * BLOCK, :] = product[
                        :, step * BLOCK : (step + 1) * BLOCK
                    ]
                    position += 1


def gram_blocks(slab):
    shape = jax.ShapeDtypeStruct((HALF_ROWS, BLOCK), jnp.float32)
    return pl.pallas_call(
        gram_kernel,
        out_shape=(shape, shape),
        in_specs=[pl.BlockSpec(memory_space=pltpu.VMEM)],
        out_specs=(pl.BlockSpec(memory_space=pltpu.VMEM),) * 2,
        compiler_params=pltpu.CompilerParams(vmem_limit_bytes=32 * 2**20),
    )(slab)


def spread(value, sublane):
    return jnp.broadcast_to(value[sublane : sublane + 1], (8, BLOCK))


def eliminate(row, offset, out):
    groups = BASE // 8
    lane = iota((8, BLOCK), 1)
    sub = iota((8, BLOCK), 0)
    result = [row[8 * group : 8 * group + 8] for group in range(groups)]

    def copied(start):
        return {
            column: [
                None
                if group < column // 8
                else jnp.broadcast_to(
                    result[group][:, offset + column : offset + column + 1], (8, BLOCK)
                )
                for group in range(groups)
            ]
            for column in range(start, start + GROUP)
        }

    pivots = [jnp.ones((8, BLOCK), jnp.float32) for _ in range(groups)]
    columns = copied(0)
    for column in range(BASE):
        home, sublane = divmod(column, 8)
        current = columns.pop(column)
        pivot = spread(current[home], sublane)
        inverse_pivot = 1.0 / pivot
        pivots[home] = jnp.where(sub == sublane, pivot, pivots[home])
        scaled = {group: current[group] * inverse_pivot for group in range(home, groups)}
        for later, values in columns.items():
            factor = spread(current[later // 8], later % 8)
            for group in range(later // 8, groups):
                values[group] = values[group] - scaled[group] * factor
        here = lane == offset + column
        source = jnp.where(here, 1.0, spread(result[home], sublane))
        for group in range(home, groups):
            if group == home:
                kept = jnp.where(here, jnp.where(sub == sublane, 1.0, 0.0), result[group])
                if sublane < 7:
                    kept = kept - jnp.where(sub > sublane, scaled[group], 0.0) * source
                result[group] = kept
            else:
                kept = jnp.where(here, 0.0, result[group])
                result[group] = kept - scaled[group] * source
        if column % GROUP == AHEAD and column - AHEAD + GROUP < BASE:
            columns.update(copied(column - AHEAD + GROUP))
        yield
    for group in range(groups):
        upper = (lane > sub + (offset + 8 * group)) & (lane < offset + BASE)
        kept = jnp.where(upper, 0.0, result[group])
        out.append(kept * lax.rsqrt(pivots[group]))


def factor_block(block, beside, beyond, out):
    count = BLOCK // BASE
    rows = [block[BASE * index : BASE * (index + 1)] for index in range(count)]
    lane = iota((BASE, BLOCK), 1)
    inverse, panel, following = [], [], None
    for index in range(count):
        done = []
        yield from eliminate(rows[index], BASE * index, done)
        done = jnp.concatenate(done, axis=0)
        start, stop = BASE * index, BASE * (index + 1)
        if index + 1 < count:
            parts = split(done)
            change = dot_tn(left_terms(parts, 0), right_terms(parts, 0))
            for later in range(index + 1, count):
                kept = jnp.where((lane >= start) & (lane < stop), 0.0, rows[later])
                rows[later] = kept - change[BASE * later : BASE * (later + 1)]
        inverse.append(jnp.where(lane < stop, done, 0.0))
        if beside is not None:
            if index == 0:
                source, following = beside(), beyond()
            piece = dot_nn(
                left_terms(split(inverse[-1][:, :stop]), 1), right_terms(split(source[:stop]), 0)
            )
            parts = split(piece)
            following = following - dot_tn(left_terms(parts, 0), right_terms(parts, 0))
            panel.append(piece)
        yield
    out.append(jnp.concatenate(inverse, axis=0))
    out.append(jnp.concatenate(panel, axis=0) if panel else None)
    out.append(following)


def weave(steps, tasks):
    count = (BLOCK // BASE) * (BASE + 1)
    done = 0
    for place, _ in enumerate(steps):
        while done < len(tasks) and done * count < (place + 1) * len(tasks):
            tasks[done]()
            done += 1
    while done < len(tasks):
        tasks[done]()
        done += 1


def block_slice(start, stop=None):
    return slice(BLOCK * start, BLOCK * (start + 1 if stop is None else stop))


def step_kernel(
    weights_ref, mine_ref, other_ref, slab_ref, out_ref, check_ref,
    matrix, panel, panel_parts, left_parts, solved, checksum, checked,
):
    low_core = lax.axis_index("core") == 0
    first, second, scale = weights_ref[0], weights_ref[1], weights_ref[2]
    identity = jnp.where(iota((BLOCK, BLOCK), 0) == iota((BLOCK, BLOCK), 1), 1.0, 0.0)
    places = {pair: divmod(place, HALF) for place, pair in enumerate(block_pairs())}
    rows_dev = slab_ref.shape[0]

    def load(row, column):
        half, place = places[row, column]
        here = block_slice(place)
        value = jnp.where(low_core == (half == 0), mine_ref[here, :], other_ref[here, :]) * scale
        matrix[block_slice(row), block_slice(column)] = value + identity if row == column else value

    def sum_rows(start, stop):
        here = block_slice(start, stop)
        total = jnp.sum(slab_ref[:, here].astype(jnp.float32), axis=0, keepdims=True)
        checksum[:, here] = total / (rows_dev**0.5)

    def keep_panel(start, value):
        here = slice(BLOCK * start, BLOCK * start + value.shape[1])
        panel[:, here] = value
        for index, part in enumerate(split(value)):
            panel_parts[block_slice(index), here] = part

    def make_panel(index, inverse_parts, start, stop):
        source = right_terms(split(matrix[block_slice(index), block_slice(start, stop)]), 0)
        keep_panel(start, dot_nn(inverse_parts, source))

    def turn_panel(row):
        for index, part in enumerate(split(panel[:, block_slice(row)].T)):
            left_parts[block_slice(row), block_slice(index)] = part

    def product(row, row_stop, start, stop):
        rows, columns = block_slice(row, row_stop), block_slice(start, stop)
        left = left_terms([left_parts[rows, block_slice(index)] for index in range(3)], 1)
        right = right_terms([panel_parts[block_slice(index), columns] for index in range(3)], 0)
        return dot_nn(left, right)

    def update_right(index, start, stop):
        rows, columns = block_slice(index + 1, stop), block_slice(start, stop)
        matrix[rows, columns] = matrix[rows, columns] - product(index + 1, stop, start, stop)

    def update_left(index, start, stop):
        change = product(index + 1, COUNT, start, stop)
        rows = block_slice(index + 1, COUNT)
        known = min(stop, index)
        width = BLOCK * (known - start)
        if known > start:
            columns = block_slice(start, known)
            matrix[rows, columns] = matrix[rows, columns] - change[:, :width]
        if stop > index:
            matrix[rows, block_slice(index)] = -change[:, width:]

    def project(index, held):
        columns = block_slice(0, index + 1)
        held.append(
            dot_nt(slab_ref[:, columns], panel_parts[:BLOCK, columns]).astype(jnp.bfloat16)
        )

    def solve(index, held, start, stop):
        columns = block_slice(start, stop)
        value = dot_nn(held[0], panel_parts[:BLOCK, columns])
        width = BLOCK * (min(stop, index) - start)
        if width > 0:
            known = solved[:, BLOCK * start : BLOCK * start + width] + value[:, :width]
            value = jnp.concatenate([known, value[:, width:]], axis=1) if stop > index else known
        if index + 1 == COUNT:
            out_ref[:, columns] = first * slab_ref[:, columns].astype(jnp.float32) + second * value
        else:
            solved[:, columns] = value

    def check(index):
        columns = block_slice(0, index + 1)
        inverse = panel[:, columns]
        weight = jnp.sum(inverse * checksum[:, columns], axis=1, keepdims=True)
        change = (inverse * weight).reshape(BLOCK // 8, 8, inverse.shape[1]).sum(axis=0)
        if index:
            known = block_slice(0, index)
            checked[:, known] = checked[:, known] + change[:, : BLOCK * index]
        checked[:, block_slice(index)] = change[:, BLOCK * index :]

    tasks = []

    def later(function, *arguments):
        tasks.append(lambda: function(*arguments))

    load(0, 0)
    for pair in places:
        if pair != (0, 0):
            later(load, *pair)
    for start in range(0, COUNT, 2):
        later(sum_rows, start, start + 2)
    diagonal = matrix[block_slice(0), block_slice(0)]
    for index in range(COUNT):
        beside = beyond = None
        if index + 1 < COUNT:
            beside = lambda at=index: matrix[block_slice(at), block_slice(at + 1)]
            beyond = lambda at=index: matrix[block_slice(at + 1), block_slice(at + 1)]
        found = []
        weave(factor_block(diagonal, beside, beyond, found), tasks)
        inverse, neighbour, diagonal = found
        inverse_parts = left_terms(split(inverse), 1)
        tasks = []
        keep_panel(index, inverse)
        if neighbour is not None:
            keep_panel(index + 1, neighbour)
            later(turn_panel, index + 1)
            start = index + 2
            while start < COUNT:
                stop = start + 2 - start % 2
                later(make_panel, index, inverse_parts, start, stop)
                for row in range(start, stop):
                    later(turn_panel, row)
                later(update_right, index, start, stop)
                start = stop
        for start in range(0, index, 2):
            later(make_panel, index, inverse_parts, start, min(start + 2, index))
        if index + 1 < COUNT:
            for start in range(0, index + 1, 2):
                later(update_left, index, start, min(start + 2, index + 1))
        held = []
        later(project, index, held)
        for start in range(0, index + 1, 2):
            later(solve, index, held, start, min(start + 2, index + 1))
        later(check, index)
    for task in tasks:
        task()
    check_ref[...] = first * checksum[...] + second * jnp.sum(checked[...], axis=0, keepdims=True)


def polar_step(weights, mine, other, slab):
    rows_dev = slab.shape[0]
    vmem = pl.BlockSpec(memory_space=pltpu.VMEM)
    return pl.pallas_call(
        step_kernel,
        out_shape=(
            jax.ShapeDtypeStruct((rows_dev, WIDTH), jnp.float32),
            jax.ShapeDtypeStruct((1, WIDTH), jnp.float32),
        ),
        in_specs=[pl.BlockSpec(memory_space=pltpu.SMEM), vmem, vmem, vmem],
        out_specs=(vmem, vmem),
        scratch_shapes=[
            pltpu.VMEM((WIDTH, WIDTH), jnp.float32),
            pltpu.VMEM((BLOCK, WIDTH), jnp.float32),
            pltpu.VMEM((3 * BLOCK, WIDTH), jnp.bfloat16),
            pltpu.VMEM((WIDTH, 3 * BLOCK), jnp.bfloat16),
            pltpu.VMEM((rows_dev, WIDTH), jnp.float32),
            pltpu.VMEM((1, WIDTH), jnp.float32),
            pltpu.VMEM((8, WIDTH), jnp.float32),
        ],
        compiler_params=pltpu.CompilerParams(vmem_limit_bytes=48 * 2**20),
    )(weights, mine, other, slab)


def exchange(parts, axis):
    return lax.all_to_all(parts, axis, 0, 0, tiled=True)


def shared(part, count):
    return jnp.broadcast_to(part[None], (count,) + part.shape)


def swap(value):
    return lax.ppermute(value, "core", [(0, 1), (1, 0)])


def sum_over_devices(mine, other):
    near = ("x", "y_low", "z_low")
    count = 1
    for name in near:
        count *= lax.axis_size(name)
    own = mine + swap(other)
    own = exchange(own.reshape(count, -1, BLOCK), near).sum(axis=0)
    for name in ("y_high", "z_high"):
        own = exchange(shared(own, lax.axis_size(name)), name).sum(axis=0)
    own = exchange(shared(own, count), near).reshape(-1, BLOCK)
    return own, swap(own)


def per_device(slab, lower_bound):
    devices_all = 1
    for name in AXES:
        devices_all *= lax.axis_size(name)
    first, second, shift = qdwh_weights(lower_bound)
    weights = jnp.stack([first, second, shift / (slab.shape[0] * devices_all)])
    mine, other = sum_over_devices(*gram_blocks(slab))
    return polar_step(weights, mine, other, slab)


def solution(mesh):
    wide = Mesh(mesh.devices.reshape(4, 2, 4, 4, 2, 2), AXES)
    return jax.shard_map(
        per_device,
        mesh=wide,
        in_specs=(P(AXES, None), P()),
        out_specs=(P(AXES, None), P(AXES, None)),
        check_vma=False,
    )
```

time: 139 us -> 120 us (0.86)
  Pallas kernels: 47.9 us -> 28.5 us
    pallas_call x1, Pallas kernels: 47.3 us -> 28 us  [polar_step(): pl.pallas_call(step_kernel, out_shape=(jax.ShapeDtypeStruct((rows_dev, WI...]
where the time goes in v3:
time: 120 us; the launch traced here: 119 us
  blocking collectives  66.5 us (55%)
  Pallas kernels  28.5 us (24%)
  starting transfers between devices  17.5 us (15%)
  waiting for transfers between devices  3.73 us (3%)
  between operations  1.63 us (1%)
    all_to_all x4, blocking collectives, exchange(): return lax.all_to_all(parts, axis, 0, 0, tiled=True)  66.5 us
    pallas_call x1, Pallas kernels, polar_step(): pl.pallas_call(step_kernel, out_shape=(jax.ShapeDtypeStruct((rows_dev, WI...  28 us
    ppermute x2, starting transfers between devices, swap(): return lax.ppermute(value, 'core', [(0, 1), (1, 0)])  17.5 us
    ppermute x2, waiting for transfers between devices, swap(): return lax.ppermute(value, 'core', [(0, 1), (1, 0)])  3.73 us
  transfers between devices with their start and end apart: 2, of which 2 were waited for; matrix products, arithmetic and copies ran while one was open for 0% of the time, Pallas kernels for 0%

profile of v3, /device:TPU:1, one launch (start us, length us, event | category | flops | bytes accessed | tf_op | source)
XLA Modules:
  0.0 119.3 jit_solution(5828361542269596806)
XLA Ops:
  0.6 0.0 copy-start
  0.6 1.0 copy-done
  1.7 0.5 shard_map.41
  2.2 8.8 %collective-permute-start = (f32[2304,128]{1,0:T(8,128)S(1)}, f32[2304,128]{1,0:T(8,128)S(1)}, u32[]{:S(2)}, u32[]{:S(2)}) collective-permute-start(f32[2304,128]{1,0:T(8,128)S(1)} %get-tuple-element.5), channel_id=1, source_target_pairs={{0,1},{1,0},{2,3},{3,2},{4,5},{5,4},{6,7},{7,6},{8,9},{9,8},{10,11... | collective-permute-start | bytes 3538952 | tf_op jit(solution)/shard_map/ppermute | solution.py:375
  11.0 2.5 %collective-permute-done = f32[2304,128]{1,0:T(8,128)S(1)} collective-permute-done((f32[2304,128]{1,0:T(8,128)S(1)}, f32[2304,128]{1,0:T(8,128)S(1)}, u32[]{:S(2)}, u32[]{:S(2)}) %collective-permute-start) | collective-permute-done | bytes 1179680 | tf_op jit(solution)/shard_map/ppermute | solution.py:375
  13.5 0.1 add.21
  13.6 19.8 %all_to_all.20 = f32[16,144,128]{2,1,0:T(8,128)S(1)} all-to-all(f32[16,144,128]{2,1,0:T(8,128)S(1)} %bitcast.8), channel_id=1, replica_groups=mesh['y_high'=4,'y_low'=2,'x'=4,'z_high'=4,'z_low'=2,'core'=2] {'x','y_l..., dimensions={0} | all-to-all | bytes 2359296 | tf_op jit(solution)/shard_map/all_to_all | solution.py:367
  33.4 0.1 reduce_sum.27
  33.5 12.7 %all_to_all.21 = f32[4,144,128]{2,1,0:T(8,128)S(1)} all-to-all(f32[4,144,128]{2,1,0:T(8,128)S(1)} %broadcast_in_dim.6), channel_id=1, replica_groups=mesh['y_high'=4,'y_low'=2,'x'=4,'z_high'=4,'z_low'=2,'core'=2] {'y_high'}, dimensions={0} | all-to-all | bytes 589824 | tf_op jit(solution)/shard_map/all_to_all | solution.py:367
  46.2 18.6 %all_to_all.22 = f32[4,144,128]{2,1,0:T(8,128)S(1)} all-to-all(f32[4,144,128]{2,1,0:T(8,128)S(1)} %broadcast_in_dim.7), channel_id=1, replica_groups=mesh['y_high'=4,'y_low'=2,'x'=4,'z_high'=4,'z_low'=2,'core'=2] {'z_high'}, dimensions={0} | all-to-all | bytes 589824 | tf_op jit(solution)/shard_map/all_to_all | solution.py:367
  64.9 0.1 broadcast_in_dim.8
  65.0 0.0 copy-start.1
  65.0 15.4 %all_to_all.23 = f32[16,144,128]{2,1,0:T(8,128)S(1)} all-to-all(f32[16,144,128]{2,1,0:T(8,128)S(1)} %broadcast_in_dim.8), channel_id=1, replica_groups=mesh['y_high'=4,'y_low'=2,'x'=4,'z_high'=4,'z_low'=2,'core'=2] {'x','y_l..., dimensions={0} | all-to-all | bytes 2359296 | tf_op jit(solution)/shard_map/all_to_all | solution.py:367
  80.4 8.7 %collective-permute-start.1 = (f32[2304,128]{1,0:T(8,128)S(1)}, f32[2304,128]{1,0:T(8,128)S(1)}, u32[]{:S(2)}, u32[]{:S(2)}) collective-permute-start(f32[2304,128]{1,0:T(8,128)S(1)} %bitcast.6), channel_id=1, source_target_pairs={{0,1},{1,0},{2,3},{3,2},{4,5},{5,4},{6,7},{7,6},{8,9},{9,8},{10,11... | collective-permute-start | bytes 3538952 | tf_op jit(solution)/shard_map/ppermute | solution.py:375
  89.9 0.1 pad_maximum_fusion.weights_ref
  90.0 1.3 %collective-permute-done.1.other_ref = f32[2304,128]{1,0:T(8,128)S(1)} collective-permute-done((f32[2304,128]{1,0:T(8,128)S(1)}, f32[2304,128]{1,0:T(8,128)S(1)}, u32[]{:S(2)}, u32[]{:S(2)}) %collective-permute-start.1) | collective-permute-done | bytes 1179680 | tf_op jit(solution)/shard_map/ppermute | solution.py:375
  91.3 0.0 copy-done.1
  91.3 28.0 %shard_map.42 = (f32[256,1024]{1,0:T(8,128)}, f32[1,1024]{1,0:T(1,128)}) custom-call(f32[3]{0:T(128)S(1)} %pad_maximum_fusion.weights_ref, f32[2304,128]{1,0:T(8,128)S(1)} %bitcast.7, f32[2304,128]{1,0:T(8,128)S(1)} %collective-permute-done.1.other_ref, bf16[256,1024]{1,0:T(8,128)(2,1)S(1)} %copy-done.1), custom_call_target="tpu_custom_call" | custom-call | tf_op jit(solution)/shard_map/pallas_call | solution.py:345
  (4 shorter events, 0.1 us)
Async XLA Ops:
  0.6 1.0 copy-start
  2.2 11.3 %collective-permute-start = (f32[2304,128]{1,0:T(8,128)S(1)}, f32[2304,128]{1,0:T(8,128)S(1)}, u32[]{:S(2)}, u32[]{:S(2)}) collective-permute-start(f32[2304,128]{1,0:T(8,128)S(1)} %get-tuple-element.5), channel_id=1, source_target_pairs={{0,1},{1,0},{2,3},{3,2},{4,5},{5,4},{6,7},{7,6},{8,9},{9,8},{10,11... | collective-permute-start | bytes 3538952 | tf_op jit(solution)/shard_map/ppermute | solution.py:375
  65.0 26.3 %copy-start.1 = (bf16[256,1024]{1,0:T(8,128)(2,1)S(1)}, bf16[256,1024]{1,0:T(8,128)(2,1)}, u32[]{:S(2)}) copy-start(bf16[256,1024]{1,0:T(8,128)(2,1)} %slab_ref.3) | copy-start | bytes 1572868
  80.4 10.9 %collective-permute-start.1 = (f32[2304,128]{1,0:T(8,128)S(1)}, f32[2304,128]{1,0:T(8,128)S(1)}, u32[]{:S(2)}, u32[]{:S(2)}) collective-permute-start(f32[2304,128]{1,0:T(8,128)S(1)} %bitcast.6), channel_id=1, source_target_pairs={{0,1},{1,0},{2,3},{3,2},{4,5},{5,4},{6,7},{7,6},{8,9},{9,8},{10,11... | collective-permute-start | bytes 3538952 | tf_op jit(solution)/shard_map/ppermute | solution.py:375

commit v4 on v3

--- a/solution.py
+++ b/solution.py
@@ -9,8 +9,7 @@
 WIDTH = 1024
 BLOCK = 128
 COUNT = WIDTH // BLOCK
-PAIRS = COUNT * (COUNT + 1) // 2
-HALF = PAIRS // 2
+HALF = (COUNT * (COUNT - 1) // 2 + COUNT // 2 + 2) // 2
 HALF_ROWS = HALF * BLOCK
 BASE = 64
 GROUP = 8
@@ -67,28 +66,45 @@
     return jnp.concatenate([high, middle, high, low, high, middle], axis=axis)
 
 
-def block_pairs():
-    return [(row, column) for row in range(COUNT) for column in range(row, COUNT)]
+def block_places():
+    names = [(row, column) for row in range(COUNT) for column in range(row + 1, COUNT)]
+    names += [(row, row) for row in range(0, COUNT, 2)] + ["diagonals", "unused"]
+    return {name: divmod(place, HALF) for place, name in enumerate(names)}
 
 
 def gram_kernel(slab_ref, mine_ref, other_ref):
     core = lax.axis_index("core")
+    across, down = iota((BLOCK, BLOCK), 1), iota((BLOCK, BLOCK), 0)
+    places = block_places()
     for side in range(2):
 
         @pl.when(core == side)
         def _():
-            position = 0
+            def keep(name, value):
+                half, place = places[name]
+                target = mine_ref if half == side else other_ref
+                target[place * BLOCK : (place + 1) * BLOCK, :] = value
+
+            even, diagonals = None, []
             for row in range(COUNT):
                 product = dot_tn(
                     slab_ref[:, row * BLOCK : (row + 1) * BLOCK], slab_ref[:, row * BLOCK :]
                 )
-                for step in range(COUNT - row):
-                    half, place = divmod(position, HALF)
-                    target = mine_ref if half == side else other_ref
-                    target[place * BLOCK : (place + 1) * BLOCK, :] = product[
-                        :, step * BLOCK : (step + 1) * BLOCK
-                    ]
-                    position += 1
+                for column in range(row + 1, COUNT):
+                    start = (column - row) * BLOCK
+                    keep((row, column), product[:, start : start + BLOCK])
+                square = product[:, :BLOCK]
+                if row % 2 == 0:
+                    even = square
+                else:
+                    keep((row - 1, row - 1), jnp.where(across >= down, even, square))
+                    on_it = jnp.where(across == down, square, 0.0)
+                    diagonals.append(jnp.sum(on_it, axis=0, keepdims=True))
+            total = jnp.zeros((BLOCK, BLOCK), jnp.float32)
+            for index, value in enumerate(diagonals):
+                total = jnp.where(down == index, value, total)
+            keep("diagonals", total)
+            keep("unused", jnp.zeros((BLOCK, BLOCK), jnp.float32))
 
 
 def gram_blocks(slab):
@@ -212,15 +228,25 @@
 ):
     low_core = lax.axis_index("core") == 0
     first, second, scale = weights_ref[0], weights_ref[1], weights_ref[2]
-    identity = jnp.where(iota((BLOCK, BLOCK), 0) == iota((BLOCK, BLOCK), 1), 1.0, 0.0)
-    places = {pair: divmod(place, HALF) for place, pair in enumerate(block_pairs())}
+    across, down = iota((BLOCK, BLOCK), 1), iota((BLOCK, BLOCK), 0)
+    identity = jnp.where(across == down, 1.0, 0.0)
+    places = block_places()
     rows_dev = slab_ref.shape[0]
 
+    def fetch(name, rows=slice(0, BLOCK)):
+        half, place = places[name]
+        here = slice(place * BLOCK + rows.start, place * BLOCK + rows.stop)
+        return jnp.where(low_core == (half == 0), mine_ref[here, :], other_ref[here, :]) * scale
+
     def load(row, column):
-        half, place = places[row, column]
-        here = block_slice(place)
-        value = jnp.where(low_core == (half == 0), mine_ref[here, :], other_ref[here, :]) * scale
-        matrix[block_slice(row), block_slice(column)] = value + identity if row == column else value
+        value = fetch((row, column))
+        if row == column:
+            turned = value.T
+            extra = fetch("diagonals", slice(row // 2, row // 2 + 1))
+            odd = jnp.where(across < down, value, jnp.where(across > down, turned, extra))
+            value = jnp.where(across >= down, value, turned) + identity
+            matrix[block_slice(row + 1), block_slice(row + 1)] = odd + identity
+        matrix[block_slice(row), block_slice(column)] = value
 
     def sum_rows(start, stop):
         here = block_slice(start, stop)
@@ -296,9 +322,9 @@
         tasks.append(lambda: function(*arguments))
 
     load(0, 0)
-    for pair in places:
-        if pair != (0, 0):
-            later(load, *pair)
+    pairs = [name for name in places if isinstance(name, tuple) and name != (0, 0)]
+    for pair in sorted(pairs):
+        later(load, *pair)
     for start in range(0, COUNT, 2):
         later(sum_rows, start, start + 2)
     diagonal = matrix[block_slice(0), block_slice(0)]

time: 120 us -> 118 us (0.983)
  blocking collectives: 66.5 us -> 65.3 us
    all_to_all x4, blocking collectives: 66.5 us -> 65.3 us  [exchange(): return lax.all_to_all(parts, axis, 0, 0, tiled=True)]
where the time goes in v4:
time: 118 us
  blocking collectives  65.3 us (55%)
  Pallas kernels  28.6 us (24%)
  starting transfers between devices  17.3 us (15%)
  waiting for transfers between devices  3.54 us (3%)
  between operations  1.63 us (1%)
    all_to_all x4, blocking collectives, exchange(): return lax.all_to_all(parts, axis, 0, 0, tiled=True)  65.3 us
    pallas_call x1, Pallas kernels, polar_step(): pl.pallas_call(step_kernel, out_shape=(jax.ShapeDtypeStruct((rows_dev, WI...  28 us
    ppermute x2, starting transfers between devices, swap(): return lax.ppermute(value, 'core', [(0, 1), (1, 0)])  17.3 us
    ppermute x2, waiting for transfers between devices, swap(): return lax.ppermute(value, 'core', [(0, 1), (1, 0)])  3.54 us
  transfers between devices with their start and end apart: 2, of which 2 were waited for; matrix products, arithmetic and copies ran while one was open for 0% of the time, Pallas kernels for 0%

profile of v4, /device:TPU:1, one launch (start us, length us, event | category | flops | bytes accessed | tf_op | source)
XLA Modules:
  0.0 117.8 jit_solution(5606074963809727920)
XLA Ops:
  0.6 0.0 copy-start
  0.6 1.0 copy-done
  1.7 0.6 shard_map.41
  2.2 8.8 %collective-permute-start = (f32[2176,128]{1,0:T(8,128)S(1)}, f32[2176,128]{1,0:T(8,128)S(1)}, u32[]{:S(2)}, u32[]{:S(2)}) collective-permute-start(f32[2176,128]{1,0:T(8,128)S(1)} %get-tuple-element.5), channel_id=1, source_target_pairs={{0,1},{1,0},{2,3},{3,2},{4,5},{5,4},{6,7},{7,6},{8,9},{9,8},{10,11... | collective-permute-start | bytes 3342344 | tf_op jit(solution)/shard_map/ppermute | solution.py:401
  11.0 2.4 %collective-permute-done = f32[2176,128]{1,0:T(8,128)S(1)} collective-permute-done((f32[2176,128]{1,0:T(8,128)S(1)}, f32[2176,128]{1,0:T(8,128)S(1)}, u32[]{:S(2)}, u32[]{:S(2)}) %collective-permute-start) | collective-permute-done | bytes 1114144 | tf_op jit(solution)/shard_map/ppermute | solution.py:401
  13.4 0.1 add.21
  13.5 19.4 %all_to_all.20 = f32[16,136,128]{2,1,0:T(8,128)S(1)} all-to-all(f32[16,136,128]{2,1,0:T(8,128)S(1)} %bitcast.8), channel_id=1, replica_groups=mesh['y_high'=4,'y_low'=2,'x'=4,'z_high'=4,'z_low'=2,'core'=2] {'x','y_l..., dimensions={0} | all-to-all | bytes 2228224 | tf_op jit(solution)/shard_map/all_to_all | solution.py:393
  32.9 0.1 reduce_sum.27
  33.0 13.1 %all_to_all.21 = f32[4,136,128]{2,1,0:T(8,128)S(1)} all-to-all(f32[4,136,128]{2,1,0:T(8,128)S(1)} %broadcast_in_dim.6), channel_id=1, replica_groups=mesh['y_high'=4,'y_low'=2,'x'=4,'z_high'=4,'z_low'=2,'core'=2] {'y_high'}, dimensions={0} | all-to-all | bytes 557056 | tf_op jit(solution)/shard_map/all_to_all | solution.py:393
  46.1 18.0 %all_to_all.22 = f32[4,136,128]{2,1,0:T(8,128)S(1)} all-to-all(f32[4,136,128]{2,1,0:T(8,128)S(1)} %broadcast_in_dim.7), channel_id=1, replica_groups=mesh['y_high'=4,'y_low'=2,'x'=4,'z_high'=4,'z_low'=2,'core'=2] {'z_high'}, dimensions={0} | all-to-all | bytes 557056 | tf_op jit(solution)/shard_map/all_to_all | solution.py:393
  64.1 0.1 broadcast_in_dim.8
  64.2 0.0 copy-start.1
  64.2 14.8 %all_to_all.23 = f32[16,136,128]{2,1,0:T(8,128)S(1)} all-to-all(f32[16,136,128]{2,1,0:T(8,128)S(1)} %broadcast_in_dim.8), channel_id=1, replica_groups=mesh['y_high'=4,'y_low'=2,'x'=4,'z_high'=4,'z_low'=2,'core'=2] {'x','y_l..., dimensions={0} | all-to-all | bytes 2228224 | tf_op jit(solution)/shard_map/all_to_all | solution.py:393
  79.0 8.5 %collective-permute-start.1 = (f32[2176,128]{1,0:T(8,128)S(1)}, f32[2176,128]{1,0:T(8,128)S(1)}, u32[]{:S(2)}, u32[]{:S(2)}) collective-permute-start(f32[2176,128]{1,0:T(8,128)S(1)} %bitcast.6), channel_id=1, source_target_pairs={{0,1},{1,0},{2,3},{3,2},{4,5},{5,4},{6,7},{7,6},{8,9},{9,8},{10,11... | collective-permute-start | bytes 3342344 | tf_op jit(solution)/shard_map/ppermute | solution.py:401
  88.5 0.1 pad_maximum_fusion.weights_ref
  88.6 1.2 %collective-permute-done.1.other_ref = f32[2176,128]{1,0:T(8,128)S(1)} collective-permute-done((f32[2176,128]{1,0:T(8,128)S(1)}, f32[2176,128]{1,0:T(8,128)S(1)}, u32[]{:S(2)}, u32[]{:S(2)}) %collective-permute-start.1) | collective-permute-done | bytes 1114144 | tf_op jit(solution)/shard_map/ppermute | solution.py:401
  89.7 0.0 copy-done.1
  89.7 28.0 %shard_map.42 = (f32[256,1024]{1,0:T(8,128)}, f32[1,1024]{1,0:T(1,128)}) custom-call(f32[3]{0:T(128)S(1)} %pad_maximum_fusion.weights_ref, f32[2176,128]{1,0:T(8,128)S(1)} %bitcast.7, f32[2176,128]{1,0:T(8,128)S(1)} %collective-permute-done.1.other_ref, bf16[256,1024]{1,0:T(8,128)(2,1)S(1)} %copy-done.1), custom_call_target="tpu_custom_call" | custom-call | tf_op jit(solution)/shard_map/pallas_call | solution.py:371
  (4 shorter events, 0.1 us)
Async XLA Ops:
  0.6 1.0 copy-start
  2.2 11.2 %collective-permute-start = (f32[2176,128]{1,0:T(8,128)S(1)}, f32[2176,128]{1,0:T(8,128)S(1)}, u32[]{:S(2)}, u32[]{:S(2)}) collective-permute-start(f32[2176,128]{1,0:T(8,128)S(1)} %get-tuple-element.5), channel_id=1, source_target_pairs={{0,1},{1,0},{2,3},{3,2},{4,5},{5,4},{6,7},{7,6},{8,9},{9,8},{10,11... | collective-permute-start | bytes 3342344 | tf_op jit(solution)/shard_map/ppermute | solution.py:401
  64.2 25.5 %copy-start.1 = (bf16[256,1024]{1,0:T(8,128)(2,1)S(1)}, bf16[256,1024]{1,0:T(8,128)(2,1)}, u32[]{:S(2)}) copy-start(bf16[256,1024]{1,0:T(8,128)(2,1)} %slab_ref.3) | copy-start | bytes 1572868
  79.0 10.7 %collective-permute-start.1 = (f32[2176,128]{1,0:T(8,128)S(1)}, f32[2176,128]{1,0:T(8,128)S(1)}, u32[]{:S(2)}, u32[]{:S(2)}) collective-permute-start(f32[2176,128]{1,0:T(8,128)S(1)} %bitcast.6), channel_id=1, source_target_pairs={{0,1},{1,0},{2,3},{3,2},{4,5},{5,4},{6,7},{7,6},{8,9},{9,8},{10,11... | collective-permute-start | bytes 3342344 | tf_op jit(solution)/shard_map/ppermute | solution.py:401

commit v5 on v4

--- a/solution.py
+++ b/solution.py
@@ -14,6 +14,8 @@
 BASE = 64
 GROUP = 8
 AHEAD = 3
+LATER = 36
+FOLLOW = 2
 AXES = ("y_high", "y_low", "x", "z_high", "z_low", "core")
 
 
@@ -122,7 +124,7 @@
     return jnp.broadcast_to(value[sublane : sublane + 1], (8, BLOCK))
 
 
-def eliminate(row, offset, out):
+def eliminate(row, offset, out, beside=None):
     groups = BASE // 8
     lane = iota((8, BLOCK), 1)
     sub = iota((8, BLOCK), 0)
@@ -143,6 +145,16 @@
 
     pivots = [jnp.ones((8, BLOCK), jnp.float32) for _ in range(groups)]
     columns = copied(0)
+    waiting = []
+    if beside is not None:
+        beside = [beside[8 * group : 8 * group + 8] for group in range(groups)]
+
+    def follow():
+        home, sublane, factors = waiting.pop(0)
+        source = spread(beside[home], sublane)
+        for group, factor in factors.items():
+            beside[group] = beside[group] - factor * source
+
     for column in range(BASE):
         home, sublane = divmod(column, 8)
         current = columns.pop(column)
@@ -160,44 +172,64 @@
             if group == home:
                 kept = jnp.where(here, jnp.where(sub == sublane, 1.0, 0.0), result[group])
                 if sublane < 7:
-                    kept = kept - jnp.where(sub > sublane, scaled[group], 0.0) * source
+                    scaled[group] = jnp.where(sub > sublane, scaled[group], 0.0)
+                    kept = kept - scaled[group] * source
+                else:
+                    del scaled[group]
                 result[group] = kept
             else:
                 kept = jnp.where(here, 0.0, result[group])
                 result[group] = kept - scaled[group] * source
         if column % GROUP == AHEAD and column - AHEAD + GROUP < BASE:
             columns.update(copied(column - AHEAD + GROUP))
+        if beside is not None:
+            waiting.append((home, sublane, scaled))
+            for _ in range(FOLLOW):
+                if column >= LATER and waiting:
+                    follow()
         yield
+    while waiting:
+        follow()
     for group in range(groups):
         upper = (lane > sub + (offset + 8 * group)) & (lane < offset + BASE)
         kept = jnp.where(upper, 0.0, result[group])
-        out.append(kept * lax.rsqrt(pivots[group]))
+        scale = lax.rsqrt(pivots[group])
+        out.append(kept * scale)
+        if beside is not None:
+            beside[group] = beside[group] * scale
+    if beside is not None:
+        out.append(jnp.concatenate(beside, axis=0))
 
 
 def factor_block(block, beside, beyond, out):
     count = BLOCK // BASE
     rows = [block[BASE * index : BASE * (index + 1)] for index in range(count)]
     lane = iota((BASE, BLOCK), 1)
-    inverse, panel, following = [], [], None
+    inverse, panel, following, below = [], [], None, None
     for index in range(count):
         done = []
-        yield from eliminate(rows[index], BASE * index, done)
+        yield from eliminate(rows[index], BASE * index, done, below)
+        piece = done.pop() if below is not None else None
         done = jnp.concatenate(done, axis=0)
         start, stop = BASE * index, BASE * (index + 1)
+        inverse.append(jnp.where(lane < stop, done, 0.0))
         if index + 1 < count:
-            parts = split(done)
-            change = dot_tn(left_terms(parts, 0), right_terms(parts, 0))
+            done_parts = split(done)
+            change = dot_tn(left_terms(done_parts, 0), right_terms(done_parts, 0))
             for later in range(index + 1, count):
                 kept = jnp.where((lane >= start) & (lane < stop), 0.0, rows[later])
                 rows[later] = kept - change[BASE * later : BASE * (later + 1)]
-        inverse.append(jnp.where(lane < stop, done, 0.0))
         if beside is not None:
             if index == 0:
                 source, following = beside(), beyond()
-            piece = dot_nn(
-                left_terms(split(inverse[-1][:, :stop]), 1), right_terms(split(source[:stop]), 0)
-            )
+                piece = dot_nn(
+                    left_terms(split(inverse[0][:, :stop]), 1),
+                    right_terms(split(source[:stop]), 0),
+                )
             parts = split(piece)
+            if index == 0:
+                change = dot_tn(left_terms(done_parts, 0), right_terms(parts, 0))
+                below = source[stop:] - change[stop:]
             following = following - dot_tn(left_terms(parts, 0), right_terms(parts, 0))
             panel.append(piece)
         yield

time: 118 us -> 118 us (level)
  no operation moved by 1% of the time
where the time goes in v5:
time: 118 us; the launch traced here: 117 us
  blocking collectives  65.3 us (55%)
  Pallas kernels  28.3 us (24%)
  starting transfers between devices  17.3 us (15%)
  waiting for transfers between devices  3.54 us (3%)
  between operations  1.63 us (1%)
    all_to_all x4, blocking collectives, exchange(): return lax.all_to_all(parts, axis, 0, 0, tiled=True)  65.3 us
    pallas_call x1, Pallas kernels, polar_step(): pl.pallas_call(step_kernel, out_shape=(jax.ShapeDtypeStruct((rows_dev, WI...  27.7 us
    ppermute x2, starting transfers between devices, swap(): return lax.ppermute(value, 'core', [(0, 1), (1, 0)])  17.3 us
    ppermute x2, waiting for transfers between devices, swap(): return lax.ppermute(value, 'core', [(0, 1), (1, 0)])  3.54 us
  transfers between devices with their start and end apart: 2, of which 2 were waited for; matrix products, arithmetic and copies ran while one was open for 0% of the time, Pallas kernels for 0%

profile of v5, /device:TPU:1, one launch (start us, length us, event | category | flops | bytes accessed | tf_op | source)
XLA Modules:
  0.0 117.5 jit_solution(5233937303157729893)
XLA Ops:
  0.6 0.0 copy-start
  0.6 1.0 copy-done
  1.7 0.6 shard_map.41
  2.2 8.8 %collective-permute-start = (f32[2176,128]{1,0:T(8,128)S(1)}, f32[2176,128]{1,0:T(8,128)S(1)}, u32[]{:S(2)}, u32[]{:S(2)}) collective-permute-start(f32[2176,128]{1,0:T(8,128)S(1)} %get-tuple-element.5), channel_id=1, source_target_pairs={{0,1},{1,0},{2,3},{3,2},{4,5},{5,4},{6,7},{7,6},{8,9},{9,8},{10,11... | collective-permute-start | bytes 3342344 | tf_op jit(solution)/shard_map/ppermute | solution.py:433
  11.0 2.4 %collective-permute-done = f32[2176,128]{1,0:T(8,128)S(1)} collective-permute-done((f32[2176,128]{1,0:T(8,128)S(1)}, f32[2176,128]{1,0:T(8,128)S(1)}, u32[]{:S(2)}, u32[]{:S(2)}) %collective-permute-start) | collective-permute-done | bytes 1114144 | tf_op jit(solution)/shard_map/ppermute | solution.py:433
  13.4 0.1 add.21
  13.5 19.4 %all_to_all.20 = f32[16,136,128]{2,1,0:T(8,128)S(1)} all-to-all(f32[16,136,128]{2,1,0:T(8,128)S(1)} %bitcast.8), channel_id=1, replica_groups=mesh['y_high'=4,'y_low'=2,'x'=4,'z_high'=4,'z_low'=2,'core'=2] {'x','y_l..., dimensions={0} | all-to-all | bytes 2228224 | tf_op jit(solution)/shard_map/all_to_all | solution.py:425
  32.9 0.1 reduce_sum.27
  33.0 13.1 %all_to_all.21 = f32[4,136,128]{2,1,0:T(8,128)S(1)} all-to-all(f32[4,136,128]{2,1,0:T(8,128)S(1)} %broadcast_in_dim.6), channel_id=1, replica_groups=mesh['y_high'=4,'y_low'=2,'x'=4,'z_high'=4,'z_low'=2,'core'=2] {'y_high'}, dimensions={0} | all-to-all | bytes 557056 | tf_op jit(solution)/shard_map/all_to_all | solution.py:425
  46.1 18.0 %all_to_all.22 = f32[4,136,128]{2,1,0:T(8,128)S(1)} all-to-all(f32[4,136,128]{2,1,0:T(8,128)S(1)} %broadcast_in_dim.7), channel_id=1, replica_groups=mesh['y_high'=4,'y_low'=2,'x'=4,'z_high'=4,'z_low'=2,'core'=2] {'z_high'}, dimensions={0} | all-to-all | bytes 557056 | tf_op jit(solution)/shard_map/all_to_all | solution.py:425
  64.1 0.1 broadcast_in_dim.8
  64.2 0.0 copy-start.1
  64.2 14.8 %all_to_all.23 = f32[16,136,128]{2,1,0:T(8,128)S(1)} all-to-all(f32[16,136,128]{2,1,0:T(8,128)S(1)} %broadcast_in_dim.8), channel_id=1, replica_groups=mesh['y_high'=4,'y_low'=2,'x'=4,'z_high'=4,'z_low'=2,'core'=2] {'x','y_l..., dimensions={0} | all-to-all | bytes 2228224 | tf_op jit(solution)/shard_map/all_to_all | solution.py:425
  79.0 8.5 %collective-permute-start.1 = (f32[2176,128]{1,0:T(8,128)S(1)}, f32[2176,128]{1,0:T(8,128)S(1)}, u32[]{:S(2)}, u32[]{:S(2)}) collective-permute-start(f32[2176,128]{1,0:T(8,128)S(1)} %bitcast.6), channel_id=1, source_target_pairs={{0,1},{1,0},{2,3},{3,2},{4,5},{5,4},{6,7},{7,6},{8,9},{9,8},{10,11... | collective-permute-start | bytes 3342344 | tf_op jit(solution)/shard_map/ppermute | solution.py:433
  88.5 0.1 pad_maximum_fusion.weights_ref
  88.6 1.2 %collective-permute-done.1.other_ref = f32[2176,128]{1,0:T(8,128)S(1)} collective-permute-done((f32[2176,128]{1,0:T(8,128)S(1)}, f32[2176,128]{1,0:T(8,128)S(1)}, u32[]{:S(2)}, u32[]{:S(2)}) %collective-permute-start.1) | collective-permute-done | bytes 1114144 | tf_op jit(solution)/shard_map/ppermute | solution.py:433
  89.7 0.0 copy-done.1
  89.7 27.7 %shard_map.42 = (f32[256,1024]{1,0:T(8,128)}, f32[1,1024]{1,0:T(1,128)}) custom-call(f32[3]{0:T(128)S(1)} %pad_maximum_fusion.weights_ref, f32[2176,128]{1,0:T(8,128)S(1)} %bitcast.7, f32[2176,128]{1,0:T(8,128)S(1)} %collective-permute-done.1.other_ref, bf16[256,1024]{1,0:T(8,128)(2,1)S(1)} %copy-done.1), custom_call_target="tpu_custom_call" | custom-call | tf_op jit(solution)/shard_map/pallas_call | solution.py:403
  (4 shorter events, 0.1 us)
Async XLA Ops:
  0.6 1.0 copy-start
  2.2 11.2 %collective-permute-start = (f32[2176,128]{1,0:T(8,128)S(1)}, f32[2176,128]{1,0:T(8,128)S(1)}, u32[]{:S(2)}, u32[]{:S(2)}) collective-permute-start(f32[2176,128]{1,0:T(8,128)S(1)} %get-tuple-element.5), channel_id=1, source_target_pairs={{0,1},{1,0},{2,3},{3,2},{4,5},{5,4},{6,7},{7,6},{8,9},{9,8},{10,11... | collective-permute-start | bytes 3342344 | tf_op jit(solution)/shard_map/ppermute | solution.py:433
  64.2 25.5 %copy-start.1 = (bf16[256,1024]{1,0:T(8,128)(2,1)S(1)}, bf16[256,1024]{1,0:T(8,128)(2,1)}, u32[]{:S(2)}) copy-start(bf16[256,1024]{1,0:T(8,128)(2,1)} %slab_ref.3) | copy-start | bytes 1572868
  79.0 10.7 %collective-permute-start.1 = (f32[2176,128]{1,0:T(8,128)S(1)}, f32[2176,128]{1,0:T(8,128)S(1)}, u32[]{:S(2)}, u32[]{:S(2)}) collective-permute-start(f32[2176,128]{1,0:T(8,128)S(1)} %bitcast.6), channel_id=1, source_target_pairs={{0,1},{1,0},{2,3},{3,2},{4,5},{5,4},{6,7},{7,6},{8,9},{9,8},{10,11... | collective-permute-start | bytes 3342344 | tf_op jit(solution)/shard_map/ppermute | solution.py:433
